TPU v7x, 128 devices: a whole 4x4x4 slice. The times are simulated.
128 devices in a mesh: mem: 64 (over z, y, x), grp: 2 (over core).
Axes of the slice: x: 4, y: 4, z: 4, core: 2. Of those that a mesh axis runs over, the one named last changes fastest.
Arguments:
- queries: bfloat16 [18432, 1024], P(('mem', 'grp')), may hold values from -2 to 2
- keys: bfloat16 [18432, 1024], P(('mem', 'grp')), may hold values from -10 to 10
- labels: int32 [18432], P(('mem', 'grp')), may hold values from 0 to 63
- memory: bfloat16 [262144, 1024], P(('mem', 'grp')), may hold values from -40 to 40
- mem_labels: int32 [262144], P(('mem', 'grp')), may hold values from 0 to 63
- pairs: int32 [2304, 3], P(('mem', 'grp')), may hold values from 0 to 127, all different within a row; in each aligned block of 18 rows (0 to 17, 18 to 35, ...) at most 2 rows name the same one
- offset: int32 [1], replicated, may hold values from 0 to 2047
Outputs:
- loss: float32 [18432], P(('mem', 'grp'))
- grad: float32 [18432, 1024], P(('mem', 'grp'))
- new_memory: bfloat16 [262144, 1024], P(('mem', 'grp'))
Inputs may be any that keep to these rules, and one draw needn't show every extreme that they name: `pairs`: each row names 3 different shards; among the 18 rows of one device no shard is named more than 2 times, and in some devices one shard exactly 2 times.
All inputs are finite; a program needn't handle non-finite values.
Results may differ from a plain program's by a relative error of at most 0.0024.
Values may be sent and summed in bfloat16 or wider, within the bound.
No kernel may reach another device: no remote copies, remote signals or barrier semaphores. Data moves between devices by JAX's collectives and lax.ppermute only.
A program may use at most 128 MiB of HBM per device.

v0:
```python
import jax
import jax.numpy as jnp
from jax import lax
from jax.sharding import PartitionSpec as P

CAP = 2


def shard_terms(rows_query, rows_label, shard_rows, shard_labels):
    scores = lax.dot_general(
        rows_query, shard_rows, (((1,), (1,)), ((), ())), preferred_element_type=jnp.float32
    )
    local_max = jnp.max(scores, axis=1)
    weights = jnp.exp(scores - local_max[:, None])
    positive = (rows_label[:, None] == shard_labels[None, :]).astype(jnp.float32)
    positive_weights = weights * positive
    part_all = jnp.sum(weights, axis=1)
    part_pos = jnp.sum(positive_weights, axis=1)
    stacked = jnp.concatenate([weights, positive_weights], axis=0).astype(jnp.bfloat16)
    sums = jnp.dot(stacked, shard_rows, preferred_element_type=jnp.float32)
    row_count = rows_query.shape[0]
    return (local_max, part_all, part_pos, sums[:row_count], sums[row_count:])


def combine(query_part, key_part, maxima, part_all, part_pos, sum_all, sum_pos):
    own_score = jnp.einsum(
        "...e,...e->...", query_part.astype(jnp.float32), key_part.astype(jnp.float32)
    )
    top_score = jnp.maximum(own_score, jnp.max(maxima, axis=-2))
    scales = jnp.exp(maxima - top_score[..., None, :])
    own_weight = jnp.exp(own_score - top_score)
    total_all = own_weight + jnp.sum(scales * part_all, axis=-2)
    total_pos = own_weight + jnp.sum(scales * part_pos, axis=-2)
    loss_rows = jnp.log(total_all) - jnp.log(total_pos)
    weighted = scales[..., None] * (
        sum_all / total_all[..., None, :, None] - sum_pos / total_pos[..., None, :, None]
    )
    own_factor = own_weight * (1.0 / total_all - 1.0 / total_pos)
    gradient = jnp.sum(weighted, axis=-3) + own_factor[..., None] * key_part.astype(jnp.float32)
    return (loss_rows, gradient)


def cycle_write(shard, shard_keys, start):
    slot_count = shard.shape[0]
    key_count = shard_keys.shape[0]
    distance = (jnp.arange(slot_count, dtype=jnp.int32) - start) % slot_count
    source = shard_keys[jnp.minimum(distance, key_count - 1)]
    return jnp.where((distance < key_count)[:, None], source, shard)


def body(queries, keys, labels, memory, mem_labels, pairs, offset):
    shards = lax.axis_size(("mem", "grp"))
    rows_dev, width = queries.shape
    block_count, fanout = pairs.shape
    block_rows = rows_dev // block_count
    capacity = CAP
    targets = pairs.reshape(-1)
    onehot = (targets[:, None] == jnp.arange(shards, dtype=jnp.int32)[None, :]).astype(jnp.int32)
    earlier = jnp.cumsum(onehot, axis=0) - onehot
    column = jnp.sum(earlier * onehot, axis=1)
    dest_slot = targets * capacity + column
    chosen_mask = jnp.arange(shards * capacity, dtype=jnp.int32)[:, None] == dest_slot[None, :]
    chosen = jnp.any(chosen_mask.reshape(shards * capacity, block_count, fanout), axis=2).astype(
        jnp.bfloat16
    )
    blocks_query = queries.reshape(block_count, block_rows * width)
    blocks_label = labels.astype(jnp.bfloat16).reshape(block_count, block_rows)
    send_query = jnp.dot(chosen, blocks_query, preferred_element_type=jnp.float32).astype(
        jnp.bfloat16
    )
    send_query = send_query.reshape(shards, capacity, block_rows, width)
    send_label = jnp.dot(chosen, blocks_label, preferred_element_type=jnp.float32).astype(
        jnp.bfloat16
    )
    send_label = send_label.reshape(shards, capacity, block_rows)
    arrived_query, arrived_label = (
        lax.all_to_all(send_query, ("mem", "grp"), split_axis=0, concat_axis=0, tiled=True),
        lax.all_to_all(send_label, ("mem", "grp"), split_axis=0, concat_axis=0, tiled=True),
    )
    total_rows = shards * capacity * block_rows
    row_step = 512
    rows_query = arrived_query.reshape(total_rows // row_step, row_step, width)
    rows_label = arrived_label.reshape(total_rows // row_step, row_step).astype(jnp.int32)

    def owner_terms(operands):
        return shard_terms(operands[0], operands[1], memory, mem_labels)

    local_max, part_all, part_pos, sum_all, sum_pos = lax.map(owner_terms, (rows_query, rows_label))
    local_max = local_max.reshape(shards, capacity, block_rows)
    part_all = part_all.reshape(shards, capacity, block_rows)
    part_pos = part_pos.reshape(shards, capacity, block_rows)
    sum_all = sum_all.reshape(shards, capacity, block_rows, width)
    sum_pos = sum_pos.reshape(shards, capacity, block_rows, width)
    query_blocks = queries.reshape(block_count, block_rows, width)
    key_blocks = keys.reshape(block_count, block_rows, width)
    returned = (
        lax.all_to_all(local_max, ("mem", "grp"), split_axis=0, concat_axis=0, tiled=True),
        lax.all_to_all(part_all, ("mem", "grp"), split_axis=0, concat_axis=0, tiled=True),
        lax.all_to_all(part_pos, ("mem", "grp"), split_axis=0, concat_axis=0, tiled=True),
        lax.all_to_all(sum_all, ("mem", "grp"), split_axis=0, concat_axis=0, tiled=True),
        lax.all_to_all(sum_pos, ("mem", "grp"), split_axis=0, concat_axis=0, tiled=True),
    )
    picked = []
    for member in range(5):
        tail_shape = returned[member].shape[-1:] if member > 2 else ()
        flat = returned[member].reshape((shards * capacity, block_rows) + tail_shape)
        picked.append(flat[dest_slot].reshape((block_count, fanout, block_rows) + tail_shape))
    loss_rows, gradient = combine(
        query_blocks, key_blocks, picked[0], picked[1], picked[2], picked[3], picked[4]
    )
    updated = cycle_write(memory, keys, offset[0])
    return (loss_rows.reshape(rows_dev), gradient.reshape(rows_dev, width), updated)


def solution(mesh):
    in_specs = (
        P(("mem", "grp"), None),
        P(("mem", "grp"), None),
        P(("mem", "grp")),
        P(("mem", "grp"), None),
        P(("mem", "grp")),
        P(("mem", "grp"), None),
        P(),
    )
    out_specs = (P(("mem", "grp")), P(("mem", "grp"), None), P(("mem", "grp"), None))
    return jax.shard_map(body, mesh=mesh, in_specs=in_specs, out_specs=out_specs, check_vma=False)
```

profile of v0, /device:TPU:1, one launch (start us, length us, event | category | flops | bytes accessed | tf_op | source)
XLA Modules:
  0.0 403.2 jit_solution(8408309229815145566)
XLA Ops:
  0.6 0.8 copy.16
  1.4 0.1 eq.47
  1.6 0.1 reduce_window_sum.11
  1.7 0.2 select_reduce_fusion
  1.8 0.1 reduce_sum.61
  1.9 0.1 copy.18
  2.0 0.1 fusion.16
  2.1 0.7 convert_element_type.29
  2.8 0.1 reshape.203
  2.9 0.2 convolution_convert_fusion.1
  3.1 0.7 copy.19
  3.8 11.5 %all-to-all-start.1 = ((bf16[128,2,8]{2,1,0:T(2,128)(2,1)}), bf16[128,2,8]{2,1,0:T(2,128)(2,1)S(1)}, u32[]{:S(2)}, u32[]{:S(2)}) async-start(bf16[128,2,8]{2,1,0:T(2,128)(2,1)} %bitcast.10), calls=%async_computation.1 | async-start | bytes 131072 | tf_op jit(solution)/shard_map/all_to_all | solution.py:78
  15.4 1.1 reshape.200
  16.5 1.3 convolution_convert_fusion
  17.8 6.3 %copy.25 = bf16[32,8,8,1024]{3,2,1,0:T(8,128)(2,1)} copy(bf16[32,8,8,1024]{3,1,2,0:T(8,128)(2,1)S(1)} %bitcast.70) | data formatting | bytes 8388608
  24.1 0.8 all-to-all-done.1
  24.9 9.5 %all-to-all-start = ((bf16[128,2,8,1024]{3,2,1,0:T(8,128)(2,1)}), bf16[128,2,8,1024]{3,2,1,0:T(8,128)(2,1)}, u32[]{:S(2)}, u32[]{:S(2)}) async-start(bf16[128,2,8,1024]{3,2,1,0:T(8,128)(2,1)} %bitcast.69), calls=%async_computation | async-start | bytes 8388608 | tf_op jit(solution)/shard_map/all_to_all | solution.py:77
  34.5 0.2 reshape.221
  34.7 52.3 %all-to-all-done = bf16[128,2,8,1024]{3,2,1,0:T(8,128)(2,1)} async-done(((bf16[128,2,8,1024]{3,2,1,0:T(8,128)(2,1)}), bf16[128,2,8,1024]{3,2,1,0:T(8,128)(2,1)}, u32[]{:S(2)}, u32[]{:S(2)}) %all-to-all-start) | async-done | bytes 4194336 | tf_op jit(solution)/shard_map/all_to_all | solution.py:77
  87.0 56.4 %while.18 = (s32[]{:T(128)}, f32[4,512]{1,0:T(4,128)S(1)}, f32[4,512]{1,0:T(4,128)S(1)}, f32[4,512]{1,0:T(4,128)S(1)}, f32[4,512,1024]{2,1,0:T(8,128)}, /*index=...) while((s32[]{:T(128)}, f32[4,512]{1,0:T(4,128)S(1)}, ...), condition=%wide.region_7.8_spmd, body=%wide.region_3.7_spmd.sunk | while | flops 6459226624 | bytes 55610528 | solution.py:88
  87.0 5.0 %fusion.48 = (f32[512]{0:T(512)S(1)}, f32[512,2048]{1,0:T(8,128)S(1)}) fusion(bf16[2048,1024]{1,0:T(8,128)(2,1)} %get-tuple-element.208, bf16[4,512,1024]{2,1,0:T(8,128)(2,1)} %get-tuple-element.207, s32[]{:T(128)} %get-tuple-element.189), kind=kOutput, calls=%fused_computation.67.clone.1 | convolution fusion | flops 2148531712 | bytes 9439744 | tf_op jit(solution)/shard_map/while/body/eval_jaxpr/dot_general | solution.py:10
  92.0 1.6 fusion.49
  93.6 0.5 copy-done.1
  94.2 4.5 %fusion.50 = f32[1024,1024]{1,0:T(8,128)S(1)} fusion(bf16[2048,1024]{1,0:T(8,128)(2,1)S(1)} %copy-done.1, bf16[512,2048]{1,0:T(8,128)(2,1)S(1)} %get-tuple-element.173, bf16[512,2048]{1,0:T(8,128)(2,1)S(1)} %get-tuple-element.174), kind=kOutput, calls=%fused_computation.6.clone.1 | convolution fusion | flops 4303355904 | bytes 12582912 | tf_op jit(solution)/shard_map/while/body/eval_jaxpr/dot_general | solution.py:20
  98.7 2.3 fusion.51
  101.1 5.0 %fusion.48 = (f32[512]{0:T(512)S(1)}, f32[512,2048]{1,0:T(8,128)S(1)}) fusion(bf16[2048,1024]{1,0:T(8,128)(2,1)} %get-tuple-element.208, bf16[4,512,1024]{2,1,0:T(8,128)(2,1)} %get-tuple-element.207, s32[]{:T(128)} %get-tuple-element.189), kind=kOutput, calls=%fused_computation.67.clone.1 | convolution fusion | flops 2148531712 | bytes 9439744 | tf_op jit(solution)/shard_map/while/body/eval_jaxpr/dot_general | solution.py:10
  106.1 1.6 fusion.49
  107.8 0.5 copy-done.1
  108.3 4.5 %fusion.50 = f32[1024,1024]{1,0:T(8,128)S(1)} fusion(bf16[2048,1024]{1,0:T(8,128)(2,1)S(1)} %copy-done.1, bf16[512,2048]{1,0:T(8,128)(2,1)S(1)} %get-tuple-element.173, bf16[512,2048]{1,0:T(8,128)(2,1)S(1)} %get-tuple-element.174), kind=kOutput, calls=%fused_computation.6.clone.1 | convolution fusion | flops 4303355904 | bytes 12582912 | tf_op jit(solution)/shard_map/while/body/eval_jaxpr/dot_general | solution.py:20
  112.8 2.3 fusion.51
  115.2 5.0 %fusion.48 = (f32[512]{0:T(512)S(1)}, f32[512,2048]{1,0:T(8,128)S(1)}) fusion(bf16[2048,1024]{1,0:T(8,128)(2,1)} %get-tuple-element.208, bf16[4,512,1024]{2,1,0:T(8,128)(2,1)} %get-tuple-element.207, s32[]{:T(128)} %get-tuple-element.189), kind=kOutput, calls=%fused_computation.67.clone.1 | convolution fusion | flops 2148531712 | bytes 9439744 | tf_op jit(solution)/shard_map/while/body/eval_jaxpr/dot_general | solution.py:10
  120.2 1.6 fusion.49
  121.9 0.5 copy-done.1
  122.4 4.5 %fusion.50 = f32[1024,1024]{1,0:T(8,128)S(1)} fusion(bf16[2048,1024]{1,0:T(8,128)(2,1)S(1)} %copy-done.1, bf16[512,2048]{1,0:T(8,128)(2,1)S(1)} %get-tuple-element.173, bf16[512,2048]{1,0:T(8,128)(2,1)S(1)} %get-tuple-element.174), kind=kOutput, calls=%fused_computation.6.clone.1 | convolution fusion | flops 4303355904 | bytes 12582912 | tf_op jit(solution)/shard_map/while/body/eval_jaxpr/dot_general | solution.py:20
  126.9 2.3 fusion.51
  129.3 5.0 %fusion.48 = (f32[512]{0:T(512)S(1)}, f32[512,2048]{1,0:T(8,128)S(1)}) fusion(bf16[2048,1024]{1,0:T(8,128)(2,1)} %get-tuple-element.208, bf16[4,512,1024]{2,1,0:T(8,128)(2,1)} %get-tuple-element.207, s32[]{:T(128)} %get-tuple-element.189), kind=kOutput, calls=%fused_computation.67.clone.1 | convolution fusion | flops 2148531712 | bytes 9439744 | tf_op jit(solution)/shard_map/while/body/eval_jaxpr/dot_general | solution.py:10
  134.3 1.6 fusion.49
  136.0 0.5 copy-done.1
  136.5 4.5 %fusion.50 = f32[1024,1024]{1,0:T(8,128)S(1)} fusion(bf16[2048,1024]{1,0:T(8,128)(2,1)S(1)} %copy-done.1, bf16[512,2048]{1,0:T(8,128)(2,1)S(1)} %get-tuple-element.173, bf16[512,2048]{1,0:T(8,128)(2,1)S(1)} %get-tuple-element.174), kind=kOutput, calls=%fused_computation.6.clone.1 | convolution fusion | flops 4303355904 | bytes 12582912 | tf_op jit(solution)/shard_map/while/body/eval_jaxpr/dot_general | solution.py:20
  141.0 2.3 fusion.51
  143.4 0.9 reshape.205
  144.3 4.3 %all-to-all-start.2 = ((f32[128,2,8]{2,1,0:T(2,128)}), f32[128,2,8]{2,1,0:T(2,128)S(1)}, u32[]{:S(2)}, u32[]{:S(2)}) async-start(f32[128,2,8]{2,1,0:T(2,128)} %reshape.205), calls=%async_computation.2 | async-start | bytes 262144 | tf_op jit(solution)/shard_map/all_to_all | solution.py:97
  148.7 0.9 reshape.208
  149.6 9.3 %all-to-all-done.2 = f32[128,2,8]{2,1,0:T(2,128)S(1)} async-done(((f32[128,2,8]{2,1,0:T(2,128)}), f32[128,2,8]{2,1,0:T(2,128)S(1)}, u32[]{:S(2)}, u32[]{:S(2)}) %all-to-all-start.2) | async-done | bytes 8224 | tf_op jit(solution)/shard_map/all_to_all | solution.py:97
  158.9 4.2 %all-to-all-start.3 = ((f32[128,2,8]{2,1,0:T(2,128)}), f32[128,2,8]{2,1,0:T(2,128)S(1)}, u32[]{:S(2)}, u32[]{:S(2)}) async-start(f32[128,2,8]{2,1,0:T(2,128)} %reshape.208), calls=%async_computation.3 | async-start | bytes 262144 | tf_op jit(solution)/shard_map/all_to_all | solution.py:98
  163.1 0.2 reshape.211
  163.3 9.8 %all-to-all-done.3 = f32[128,2,8]{2,1,0:T(2,128)S(1)} async-done(((f32[128,2,8]{2,1,0:T(2,128)}), f32[128,2,8]{2,1,0:T(2,128)S(1)}, u32[]{:S(2)}, u32[]{:S(2)}) %all-to-all-start.3) | async-done | bytes 8224 | tf_op jit(solution)/shard_map/all_to_all | solution.py:98
  173.1 14.1 %all_to_all.35 = f32[128,2,8]{2,1,0:T(2,128)S(1)} all-to-all(f32[128,2,8]{2,1,0:T(2,128)S(1)} %reshape.211), channel_id=1, replica_groups=mesh['mem'=64,'grp'=2] {'mem','grp'}, dimensions={0} | all-to-all | bytes 16384 | tf_op jit(solution)/shard_map/all_to_all | solution.py:99
  187.2 103.2 %all_to_all.36 = f32[128,2,8,1024]{3,2,1,0:T(8,128)} all-to-all(f32[128,2,8,1024]{3,2,1,0:T(8,128)} %bitcast.72), channel_id=1, replica_groups=mesh['mem'=64,'grp'=2] {'mem','grp'}, dimensions={0} | all-to-all | bytes 16777216 | tf_op jit(solution)/shard_map/all_to_all | solution.py:100
  290.4 5.7 %all-to-all-start.6 = ((f32[128,2,8,1024]{3,2,1,0:T(8,128)}), f32[128,2,8,1024]{3,2,1,0:T(8,128)}, u32[]{:S(2)}, u32[]{:S(2)}) async-start(f32[128,2,8,1024]{3,2,1,0:T(8,128)} %bitcast.73), calls=%async_computation.6 | async-start | bytes 16777216 | tf_op jit(solution)/shard_map/all_to_all | solution.py:101
  296.1 0.1 mul.57
  297.0 9.6 %gather_fusion.5 = bf16[2048,1024]{1,0:T(8,128)(2,1)} fusion(bf16[144,1024]{1,0:T(8,128)(2,1)S(1)} %copy-done, s32[2048]{0:T(1024)S(1)} %broadcast_clamp_fusion), kind=kCustom, calls=%fused_computation.5 | custom fusion | bytes 8396800 | tf_op jit(solution)/shard_map/gather | solution.py:47
  306.6 0.2 fusion.15
  306.8 5.1 %broadcast_select_fusion = bf16[2048,1024]{1,0:T(8,128)(2,1)} fusion(bf16[2048,1024]{1,0:T(8,128)(2,1)} %gather_fusion.5, bf16[2048,1024]{1,0:T(8,128)(2,1)} %get-tuple-element.217, pred[2048]{0:T(1024)(128)(4,1)S(1)} %fusion.19), kind=kLoop, calls=%fused_computation.27 | loop fusion | flops 2097152 | bytes 12584960 | tf_op jit(solution)/shard_map/jit(_where)/select_n | solution.py:48
  311.9 0.6 gather_fusion
  312.5 0.6 gather_fusion.1
  313.1 0.6 gather_fusion.2
  313.9 0.1 mul.63
  314.0 0.7 reshape.214
  314.6 4.0 %gather_fusion.3 = f32[54,8,1024]{2,1,0:T(8,128)S(1)} fusion(f32[256,8,1024]{2,1,0:T(8,128)} %bitcast.71, s32[1024]{0:T(1024)S(1)} %pad_clamp_fusion), kind=kCustom, calls=%fused_computation.3 | custom fusion | bytes 3539160 | tf_op jit(solution)/shard_map/gather | solution.py:107
  318.7 76.3 %all-to-all-done.6 = f32[128,2,8,1024]{3,2,1,0:T(8,128)} async-done(((f32[128,2,8,1024]{3,2,1,0:T(8,128)}), f32[128,2,8,1024]{3,2,1,0:T(8,128)}, u32[]{:S(2)}, u32[]{:S(2)}) %all-to-all-start.6) | async-done | bytes 8388640 | tf_op jit(solution)/shard_map/all_to_all | solution.py:101
  395.0 5.3 %gather_fusion.4 = f32[54,8,1024]{2,1,0:T(8,128)} fusion(f32[256,8,1024]{2,1,0:T(8,128)} %bitcast.20, s32[1024]{0:T(1024)S(1)} %pad_clamp_fusion), kind=kCustom, calls=%fused_computation.4 | custom fusion | bytes 3539160 | tf_op jit(solution)/shard_map/gather | solution.py:107
  400.3 1.9 multiply_reduce_fusion
  402.2 0.9 bitcast_add_fusion
  (47 shorter events, 1.0 us)
Async XLA Ops:
  3.8 21.0 %all-to-all-start.1 = ((bf16[128,2,8]{2,1,0:T(2,128)(2,1)}), bf16[128,2,8]{2,1,0:T(2,128)(2,1)S(1)}, u32[]{:S(2)}, u32[]{:S(2)}) async-start(bf16[128,2,8]{2,1,0:T(2,128)(2,1)} %bitcast.10), calls=%async_computation.1 | async-start | bytes 131072 | tf_op jit(solution)/shard_map/all_to_all | solution.py:78
  24.9 62.1 %copy-start.3 = (s32[2048]{0:T(1024)S(1)}, s32[2048]{0:T(1024)}, u32[]{:S(2)}) copy-start(s32[2048]{0:T(1024)} %param.13) | copy-start | bytes 24580
  24.9 62.1 %all-to-all-start = ((bf16[128,2,8,1024]{3,2,1,0:T(8,128)(2,1)}), bf16[128,2,8,1024]{3,2,1,0:T(8,128)(2,1)}, u32[]{:S(2)}, u32[]{:S(2)}) async-start(bf16[128,2,8,1024]{3,2,1,0:T(8,128)(2,1)} %bitcast.69), calls=%async_computation | async-start | bytes 8388608 | tf_op jit(solution)/shard_map/all_to_all | solution.py:77
  92.0 2.2 copy-start.1
  106.1 2.2 copy-start.1
  120.2 2.2 copy-start.1
  134.3 2.2 copy-start.1
  144.3 14.5 %all-to-all-start.2 = ((f32[128,2,8]{2,1,0:T(2,128)}), f32[128,2,8]{2,1,0:T(2,128)S(1)}, u32[]{:S(2)}, u32[]{:S(2)}) async-start(f32[128,2,8]{2,1,0:T(2,128)} %reshape.205), calls=%async_computation.2 | async-start | bytes 262144 | tf_op jit(solution)/shard_map/all_to_all | solution.py:97
  158.9 14.2 %all-to-all-start.3 = ((f32[128,2,8]{2,1,0:T(2,128)}), f32[128,2,8]{2,1,0:T(2,128)S(1)}, u32[]{:S(2)}, u32[]{:S(2)}) async-start(f32[128,2,8]{2,1,0:T(2,128)} %reshape.208), calls=%async_computation.3 | async-start | bytes 262144 | tf_op jit(solution)/shard_map/all_to_all | solution.py:98
  290.4 6.5 %copy-start = (bf16[144,1024]{1,0:T(8,128)(2,1)S(1)}, bf16[144,1024]{1,0:T(8,128)(2,1)}, u32[]{:S(2)}) copy-start(bf16[144,1024]{1,0:T(8,128)(2,1)} %param.10) | copy-start | bytes 884740
  290.4 104.5 %all-to-all-start.6 = ((f32[128,2,8,1024]{3,2,1,0:T(8,128)}), f32[128,2,8,1024]{3,2,1,0:T(8,128)}, u32[]{:S(2)}, u32[]{:S(2)}) async-start(f32[128,2,8,1024]{3,2,1,0:T(8,128)} %bitcast.73), calls=%async_computation.6 | async-start | bytes 16777216 | tf_op jit(solution)/shard_map/all_to_all | solution.py:101
  297.0 9.7 %copy-start.2 = (bf16[144,1024]{1,0:T(8,128)(2,1)S(1)}, bf16[144,1024]{1,0:T(8,128)(2,1)}, u32[]{:S(2)}) copy-start(bf16[144,1024]{1,0:T(8,128)(2,1)} %param.9) | copy-start | bytes 884740
where the time goes:
time: 408 us; the launch traced here: 403 us
  waiting for transfers between devices  148 us (36%)
  blocking collectives  117 us (29%)
  local copies, waits for them, and re-layouts  45.1 us (11%)
  matrix products  39.3 us (10%)
  starting transfers between devices  35.2 us (9%)
  other arithmetic  16 us (4%)
    all_to_all x1, blocking collectives, body(): lax.all_to_all(sum_all, ('mem', 'grp'), split_axis=0, concat_axis=0, tile...  103 us
    all_to_all x1, waiting for transfers between devices, body(): lax.all_to_all(sum_pos, ('mem', 'grp'), split_axis=0, concat_axis=0, tile...  76.3 us
    all_to_all x1, waiting for transfers between devices, body(): lax.all_to_all(send_query, ('mem', 'grp'), split_axis=0, concat_axis=0, t...  52.3 us
    dot_general x4, matrix products, shard_terms(): lax.dot_general(rows_query, shard_rows, (((1,), (1,)), ((), ())), preferr...  19.9 us
    dot_general x4, matrix products, shard_terms(): sums = jnp.dot(stacked, shard_rows, preferred_element_type=jnp.float32)  18 us
    all_to_all x1, blocking collectives, body(): lax.all_to_all(part_pos, ('mem', 'grp'), split_axis=0, concat_axis=0, til...  14.1 us
    all_to_all x1, starting transfers between devices, body(): lax.all_to_all(send_label, ('mem', 'grp'), split_axis=0, concat_axis=0, t...  11.5 us
    gather x5, local copies, waits for them, and re-layouts, body(): flat[dest_slot].reshape((block_count, fanout, block_rows) + tail_shape)  11.1 us
  transfers between devices with their start and end apart: 5, of which 5 were waited for; matrix products, arithmetic and copies ran while one was open for 8% of the time, Pallas kernels for 0%

commit v1 on v0

v1 whole, which is shorter than its diff:
```python
import jax
import jax.numpy as jnp
from jax import lax
from jax.experimental import pallas as pl
from jax.experimental.pallas import tpu as pltpu
from jax.sharding import PartitionSpec as P

CAP = 2
F32 = jnp.float32
BF16 = jnp.bfloat16
I32 = jnp.int32
AXES = ("mem", "grp")
LANES = 128
VMEM = 56 * 1024 * 1024
EXACT = lax.Precision.HIGHEST


def iota(shape, axis):
    return lax.broadcasted_iota(I32, shape, axis)


def targets(pairs_ref, k, block_of):
    out = jnp.zeros(block_of.shape, I32)
    for b in range(pairs_ref.shape[0]):
        out = jnp.where(block_of == b, pairs_ref[b, k], out)
    return out


def spread(packed, rows):
    n = packed.shape[0]
    return jnp.broadcast_to(packed[:, None, :], (n, 16, LANES)).reshape(rows, LANES)


def column_of(wide, group):
    rows = wide.shape[0]
    pick = iota((rows, LANES), 1) == group * 16 + (iota((rows, LANES), 0) & 15)
    return jnp.sum(jnp.where(pick, wide, 0.0), axis=1, keepdims=True)


def pack_kernel(pairs_ref, label_ref, query_ref, send_ref, send_label_ref):
    step = pl.program_id(0)
    rows_dev = query_ref.shape[0]
    fanout = pairs_ref.shape[1]
    lane = iota((1, rows_dev), 1)
    shard = iota((16, rows_dev), 0) + step * 16
    match = jnp.zeros((16, rows_dev), jnp.bool_)
    for k in range(fanout):
        match = match | (targets(pairs_ref, k, lane >> 3) == shard)
    match_f = match.astype(F32)
    before = (iota((rows_dev, rows_dev), 0) >> 3) < (iota((rows_dev, rows_dev), 1) >> 3)
    before = before & ((iota((rows_dev, rows_dev), 0) & 7) == 0)
    earlier = jnp.dot(match_f.astype(BF16), before.astype(F32).astype(BF16), preferred_element_type=F32)
    first = jnp.where(earlier < 0.5, match_f, 0.0)
    second = match_f - first
    place = iota((16, 16, rows_dev), 1)
    chosen = jnp.where(place < 8, first[:, None, :], second[:, None, :])
    chosen = jnp.where((place & 7) == (iota((16, 16, rows_dev), 2) & 7), chosen, 0.0)
    chosen_rows = chosen.reshape(256, rows_dev).astype(BF16)
    send_ref[...] = jnp.dot(chosen_rows, query_ref[...], preferred_element_type=F32).astype(BF16)
    row_label = jnp.sum(chosen * label_ref[...][None].astype(F32), axis=2)
    send_label_ref[...] = jnp.concatenate([row_label, jnp.zeros((16, LANES - 16), F32)], axis=1)


def pack(pairs, labels, queries, shards):
    rows_dev, width = queries.shape
    return pl.pallas_call(
        pack_kernel,
        grid=(shards // 16,),
        in_specs=[
            pl.BlockSpec(memory_space=pltpu.SMEM),
            pl.BlockSpec((1, rows_dev), lambda i: (0, 0)),
            pl.BlockSpec((rows_dev, width), lambda i: (0, 0)),
        ],
        out_specs=[
            pl.BlockSpec((256, width), lambda i: (i, 0)),
            pl.BlockSpec((16, LANES), lambda i: (i, 0)),
        ],
        out_shape=[
            jax.ShapeDtypeStruct((shards * 16, width), BF16),
            jax.ShapeDtypeStruct((shards, LANES), F32),
        ],
        compiler_params=pltpu.CompilerParams(vmem_limit_bytes=VMEM),
        name="pack",
    )(pairs, labels.reshape(1, rows_dev), queries)


def score_kernel(query_ref, label_ref, memory_ref, slot_label_ref, weight_ref, stat_ref):
    rows = query_ref.shape[0]
    scores = lax.dot_general(
        query_ref[...], memory_ref[...], (((1,), (1,)), ((), ())), preferred_element_type=F32
    )
    top = jnp.max(scores, axis=1, keepdims=True)
    weights = jnp.exp(scores - top)
    row_label = column_of(spread(label_ref[...], rows), 0)
    same = row_label == slot_label_ref[...].astype(F32)
    part_all = jnp.sum(weights, axis=1, keepdims=True)
    part_pos = jnp.sum(jnp.where(same, weights, 0.0), axis=1, keepdims=True)
    weight_ref[...] = weights.astype(BF16)
    lane = iota((rows, LANES), 1)
    place = iota((rows, LANES), 0) & 15
    wide = jnp.where(lane == place, top, 0.0)
    wide = jnp.where(lane == place + 16, part_all, wide)
    wide = jnp.where(lane == place + 32, part_pos, wide)
    stat_ref[...] = jnp.sum(wide.reshape(rows // 16, 16, LANES), axis=1)


def score(rows_query, rows_label, memory, slot_label):
    total, width = rows_query.shape
    slots = memory.shape[0]
    step = 256
    return pl.pallas_call(
        score_kernel,
        grid=(total // step,),
        in_specs=[
            pl.BlockSpec((step, width), lambda i: (i, 0)),
            pl.BlockSpec((step // 16, LANES), lambda i: (i, 0)),
            pl.BlockSpec((slots, width), lambda i: (0, 0)),
            pl.BlockSpec((1, slots), lambda i: (0, 0)),
        ],
        out_specs=[
            pl.BlockSpec((step, slots), lambda i: (i, 0)),
            pl.BlockSpec((step // 16, LANES), lambda i: (i, 0)),
        ],
        out_shape=[
            jax.ShapeDtypeStruct((total, slots), BF16),
            jax.ShapeDtypeStruct((total // 16, LANES), F32),
        ],
        compiler_params=pltpu.CompilerParams(vmem_limit_bytes=VMEM),
        cost_estimate=pl.CostEstimate(
            flops=2 * total * slots * width, bytes_accessed=16 << 20, transcendentals=total * slots
        ),
        name="score",
    )(rows_query, rows_label, memory, slot_label)


def sums_kernel(weight_ref, label_ref, memory_ref, slot_label_ref, all_ref, pos_ref):
    rows = weight_ref.shape[0]
    weights = weight_ref[...]
    row_label = column_of(spread(label_ref[...], rows), 0)
    same = row_label == slot_label_ref[...].astype(F32)
    positive = jnp.where(same, weights.astype(F32), 0.0).astype(BF16)
    rows_memory = memory_ref[...]
    all_ref[...] = jnp.dot(weights, rows_memory, preferred_element_type=F32)
    pos_ref[...] = jnp.dot(positive, rows_memory, preferred_element_type=F32)


def sums(weights, rows_label, memory, slot_label, first, count):
    slots, width = memory.shape
    step = 256
    lead = first // step
    return pl.pallas_call(
        sums_kernel,
        grid=(count // step,),
        in_specs=[
            pl.BlockSpec((step, slots), lambda i: (i + lead, 0)),
            pl.BlockSpec((step // 16, LANES), lambda i: (i + lead, 0)),
            pl.BlockSpec((slots, width), lambda i: (0, 0)),
            pl.BlockSpec((1, slots), lambda i: (0, 0)),
        ],
        out_specs=[
            pl.BlockSpec((step, width), lambda i: (i, 0)),
            pl.BlockSpec((step, width), lambda i: (i, 0)),
        ],
        out_shape=[jax.ShapeDtypeStruct((count, width), F32)] * 2,
        compiler_params=pltpu.CompilerParams(vmem_limit_bytes=VMEM),
        cost_estimate=pl.CostEstimate(
            flops=4 * count * slots * width, bytes_accessed=16 << 20, transcendentals=0
        ),
        name="sums",
    )(weights, rows_label, memory, slot_label)


def total_kernel(pairs_ref, query_ref, key_ref, stat_ref, loss_ref, factor_ref, back_ref):
    rows = query_ref.shape[0]
    fanout = pairs_ref.shape[1]
    own = jnp.sum(query_ref[...].astype(F32) * key_ref[...].astype(F32), axis=1, keepdims=True)
    stat = stat_ref[...]
    stat_slot = (iota(stat.shape, 1) >> 3) & 1

    down_block = iota((rows, 1), 0) >> 3
    down_match = [
        (targets(pairs_ref, k, down_block) == iota((rows, LANES), 1)).astype(F32) for k in range(fanout)
    ]
    side = (rows, rows)
    earlier_down = ((iota(side, 1) >> 3) < (iota(side, 0) >> 3)) & ((iota(side, 1) & 7) == 0)
    down_count = jnp.dot(
        earlier_down.astype(F32).astype(BF16),
        sum(down_match[1:], down_match[0]).astype(BF16),
        preferred_element_type=F32,
    )
    lane = iota((rows, LANES), 1)
    mine = (lane & 7) == (iota((rows, LANES), 0) & 7)
    maxima, alls, poss = [], [], []
    for k in range(fanout):
        wide = jnp.zeros((rows, LANES), F32)
        for s in range(CAP):
            mask = jnp.where(down_count == s, down_match[k], 0.0)
            wide = wide + jnp.dot(
                mask, jnp.where(stat_slot == s, stat, 0.0), precision=EXACT, preferred_element_type=F32
            )
        for group, into in enumerate((maxima, alls, poss)):
            pick = mine & ((lane >> 4) == group)
            into.append(jnp.sum(jnp.where(pick, wide, 0.0), axis=1, keepdims=True))
    top = own
    for value in maxima:
        top = jnp.maximum(top, value)
    own_weight = jnp.exp(own - top)
    scales = [jnp.exp(value - top) for value in maxima]
    total_all, total_pos = own_weight, own_weight
    for k in range(fanout):
        total_all = total_all + scales[k] * alls[k]
        total_pos = total_pos + scales[k] * poss[k]
    loss = jnp.log(total_all) - jnp.log(total_pos)
    loss_ref[...] = jnp.sum(jnp.where(iota(side, 0) == iota(side, 1), loss, 0.0), axis=0, keepdims=True)
    factor_ref[...] = own_weight * (1.0 / total_all - 1.0 / total_pos)

    across_block = iota((1, rows), 1) >> 3
    across_match = [
        (targets(pairs_ref, k, across_block) == iota((LANES, rows), 0)).astype(F32) for k in range(fanout)
    ]
    earlier_across = ((iota(side, 0) >> 3) < (iota(side, 1) >> 3)) & ((iota(side, 0) & 7) == 0)
    across_count = jnp.dot(
        sum(across_match[1:], across_match[0]).astype(BF16),
        earlier_across.astype(F32).astype(BF16),
        preferred_element_type=F32,
    )
    back = jnp.zeros((LANES, LANES), F32)
    for k in range(fanout):
        factor_all, factor_pos = scales[k] / total_all, scales[k] / total_pos
        for s in range(CAP):
            mask = jnp.where(across_count == s, across_match[k], 0.0)
            value = jnp.where((lane >> 3) == s, factor_all, 0.0)
            value = jnp.where((lane >> 3) == 2 + s, factor_pos, value)
            value = jnp.where(mine, value, 0.0)
            back = back + jnp.dot(mask, value, precision=EXACT, preferred_element_type=F32)
    back_ref[...] = back


def totals(pairs, queries, keys, stat):
    rows = queries.shape[0]
    return pl.pallas_call(
        total_kernel,
        in_specs=[pl.BlockSpec(memory_space=pltpu.SMEM)] + [pl.BlockSpec(memory_space=pltpu.VMEM)] * 3,
        out_specs=[pl.BlockSpec(memory_space=pltpu.VMEM)] * 3,
        out_shape=[
            jax.ShapeDtypeStruct((1, rows), F32),
            jax.ShapeDtypeStruct((rows, 1), F32),
            jax.ShapeDtypeStruct(stat.shape, F32),
        ],
        compiler_params=pltpu.CompilerParams(vmem_limit_bytes=VMEM),
        name="totals",
    )(pairs, queries, keys, stat)


def merge_kernel(halves, factor_ref, *refs):
    out_ref = refs[-1]
    rows = out_ref.shape[0]
    wide = spread(factor_ref[...], rows)
    factor_all, factor_pos = column_of(wide, 0), column_of(wide, 1)
    step = pl.program_id(0)
    per = pl.num_programs(0) // halves
    for h in range(halves):

        @pl.when(step // per == h)
        def _():
            out_ref[...] = (
                factor_all * refs[2 * h][...] - factor_pos * refs[2 * h + 1][...]
            ).astype(BF16)


def merge(factors, parts):
    halves = len(parts)
    count, width = parts[0][0].shape
    step = 256
    per = count // step

    def place(h):
        return lambda i: (jnp.clip(i - h * per, 0, per - 1), 0)

    def kernel(*refs):
        merge_kernel(halves, *refs)

    return pl.pallas_call(
        kernel,
        grid=(halves * per,),
        in_specs=[pl.BlockSpec((step // 16, LANES), lambda i: (i, 0))]
        + [pl.BlockSpec((step, width), place(h)) for h in range(halves) for _ in range(2)],
        out_specs=pl.BlockSpec((step, width), lambda i: (i, 0)),
        out_shape=jax.ShapeDtypeStruct((halves * count, width), BF16),
        compiler_params=pltpu.CompilerParams(vmem_limit_bytes=VMEM),
        name="merge",
    )(factors, *[array for part in parts for array in part])


def gradient_kernel(pairs_ref, factor_ref, key_ref, back_ref, out_ref):
    step = pl.program_id(0)
    rows = key_ref.shape[0]
    chunk = back_ref.shape[0]
    block = iota((rows, 1), 0) >> 3
    place = iota((rows, chunk), 1) + step * chunk
    match = jnp.zeros((rows, chunk), F32)
    for k in range(pairs_ref.shape[1]):
        match = jnp.where(targets(pairs_ref, k, block) == (place >> 4), 1.0, match)
    side = (rows, rows)
    earlier = ((iota(side, 1) >> 3) < (iota(side, 0) >> 3)) & ((iota(side, 1) & 7) == 0)
    count = jnp.dot(earlier.astype(F32).astype(BF16), match.astype(BF16), preferred_element_type=F32)
    chosen = jnp.where(count == ((place >> 3) & 1).astype(F32), match, 0.0)
    chosen = jnp.where((place & 7) == (iota((rows, chunk), 0) & 7), chosen, 0.0)

    @pl.when(step == 0)
    def _():
        out_ref[...] = factor_ref[...] * key_ref[...].astype(F32)

    out_ref[...] += jnp.dot(chosen.astype(BF16), back_ref[...], preferred_element_type=F32)


def gradient(pairs, factor, keys, back):
    rows, width = keys.shape
    total = back.shape[0]
    chunk = 512
    return pl.pallas_call(
        gradient_kernel,
        grid=(total // chunk,),
        in_specs=[
            pl.BlockSpec(memory_space=pltpu.SMEM),
            pl.BlockSpec((rows, 1), lambda i: (0, 0)),
            pl.BlockSpec((rows, width), lambda i: (0, 0)),
            pl.BlockSpec((chunk, width), lambda i: (i, 0)),
        ],
        out_specs=pl.BlockSpec((rows, width), lambda i: (0, 0)),
        out_shape=jax.ShapeDtypeStruct((rows, width), F32),
        compiler_params=pltpu.CompilerParams(vmem_limit_bytes=VMEM),
        name="gradient",
    )(pairs, factor, keys, back)


def enqueue_kernel(slots, offset_ref, key_ref, memory_ref, out_ref):
    rows = memory_ref.shape[0]
    count = key_ref.shape[0]
    distance = iota((rows, 1), 0) + (pl.program_id(0) * rows - offset_ref[0] + slots)
    distance = jnp.where(distance >= slots, distance - slots, distance)
    lead = lax.rem(pl.program_id(0) * rows - offset_ref[0] + slots, slots)
    out_ref[...] = memory_ref[...]

    @pl.when((lead < count) | (lead + rows > slots))
    def _():
        pick = (distance == iota((rows, count), 1)).astype(F32).astype(BF16)
        fresh = jnp.dot(pick, key_ref[...], preferred_element_type=F32)
        out_ref[...] = jnp.where(distance < count, fresh, memory_ref[...].astype(F32)).astype(BF16)


def enqueue(offset, keys, memory):
    slots, width = memory.shape
    count = keys.shape[0]
    step = 256

    def kernel(*refs):
        enqueue_kernel(slots, *refs)

    return pl.pallas_call(
        kernel,
        grid=(slots // step,),
        in_specs=[
            pl.BlockSpec(memory_space=pltpu.SMEM),
            pl.BlockSpec((count, width), lambda i: (0, 0)),
            pl.BlockSpec((step, width), lambda i: (i, 0)),
        ],
        out_specs=pl.BlockSpec((step, width), lambda i: (i, 0)),
        out_shape=jax.ShapeDtypeStruct((slots, width), BF16),
        compiler_params=pltpu.CompilerParams(vmem_limit_bytes=VMEM),
        name="enqueue",
    )(offset, keys, memory)


def exchange(rows, per):
    shards = lax.axis_size(AXES)
    grouped = rows.reshape(shards, per, rows.shape[1])
    moved = lax.all_to_all(grouped, AXES, split_axis=0, concat_axis=0, tiled=True)
    return moved.reshape(rows.shape)


def body(queries, keys, labels, memory, mem_labels, pairs, offset):
    shards = lax.axis_size(AXES)
    rows_dev, width = queries.shape
    slots = memory.shape[0]
    slot_label = mem_labels.reshape(1, slots)
    send_query, send_label = pack(pairs, labels, queries, shards)
    rows_label = exchange(send_label, 1)
    rows_query = exchange(send_query, 16)
    updated = enqueue(offset, keys, memory)
    weights, stat = score(rows_query, rows_label, memory, slot_label)
    half = shards * 8
    stat = exchange(stat, 1)
    parts = [sums(weights, rows_label, memory, slot_label, first, half) for first in (0, half)]
    loss, factor, factors = totals(pairs, queries, keys, stat)
    factors = exchange(factors, 1)
    back = exchange(merge(factors, parts), 16)
    grad = gradient(pairs, factor, keys, back)
    return loss.reshape(rows_dev), grad, updated


def solution(mesh):
    in_specs = (
        P(AXES, None),
        P(AXES, None),
        P(AXES),
        P(AXES, None),
        P(AXES),
        P(AXES, None),
        P(),
    )
    out_specs = (P(AXES), P(AXES, None), P(AXES, None))
    return jax.shard_map(body, mesh=mesh, in_specs=in_specs, out_specs=out_specs, check_vma=False)
```

time: 408 us -> 233 us (0.57)
  waiting for transfers between devices: 148 us -> 45 us
  Pallas kernels: 0 us -> 78.7 us
  local copies, waits for them, and re-layouts: 45.1 us -> 2.61 us
  matrix products: 39.3 us -> 0 us
  blocking collectives: 117 us -> 79.9 us
  other arithmetic: 16 us -> 0 us
  starting transfers between devices: 35.2 us -> 24.4 us
    all_to_all x5 -> x3, waiting for transfers between devices: 148 us -> 45 us  [exchange(): lax.all_to_all(grouped, AXES, split_axis=0, concat_axis=0, tiled=True)]
    pallas_call x0 -> x8, Pallas kernels: none -> 78.7 us  [the longest x2 25.9 us: sums(): pl.pallas_call(sums_kernel, grid=(count // step,), in_specs=[pl.BlockSpec...]
    dot_general x10 -> x0, matrix products: 39.3 us -> none  [the longest x4 19.9 us: shard_terms(): lax.dot_general(rows_query, shard_rows, (((1,), (1,)), ((), ())), preferr...]
    all_to_all x2, blocking collectives: 117 us -> 79.9 us  [exchange(): lax.all_to_all(grouped, AXES, split_axis=0, concat_axis=0, tiled=True)]
    gather x6 -> x0, local copies, waits for them, and re-layouts: 20.7 us -> none  [the longest x5 11.1 us: body(): flat[dest_slot].reshape((block_count, fanout, block_rows) + tail_shape)]
    all_to_all x5 -> x3, starting transfers between devices: 35.2 us -> 24.4 us  [exchange(): lax.all_to_all(grouped, AXES, split_axis=0, concat_axis=0, tiled=True)]
    dynamic_update_slice x16 -> x0, local copies, waits for them, and re-layouts: 9.66 us -> none  [body(): lax.map(owner_terms, (rows_query, rows_label))]
    reduce_sum x7 -> x0, other arithmetic: 8.69 us -> none  [the longest x4 6.5 us: shard_terms(): part_pos = jnp.sum(positive_weights, axis=1)]
  transfers between devices with their start and end apart: 5 -> 3, of which waited for: 5 -> 1; matrix products, arithmetic and copies ran while one was open for 8% -> 0% of each run, Pallas kernels for 0% -> 14%
where the time goes in v1:
time: 233 us; the launch traced here: 232 us
  blocking collectives  79.9 us (34%)
  Pallas kernels  78.7 us (34%)
  waiting for transfers between devices  45 us (19%)
  starting transfers between devices  24.4 us (10%)
  local copies, waits for them, and re-layouts  2.61 us (1%)
    all_to_all x2, blocking collectives, exchange(): lax.all_to_all(grouped, AXES, split_axis=0, concat_axis=0, tiled=True)  79.9 us
    all_to_all x3, waiting for transfers between devices, exchange(): lax.all_to_all(grouped, AXES, split_axis=0, concat_axis=0, tiled=True)  45 us
    pallas_call x2, Pallas kernels, sums(): pl.pallas_call(sums_kernel, grid=(count // step,), in_specs=[pl.BlockSpec...  25.9 us
    all_to_all x3, starting transfers between devices, exchange(): lax.all_to_all(grouped, AXES, split_axis=0, concat_axis=0, tiled=True)  24.4 us
    pallas_call x1, Pallas kernels, score(): pl.pallas_call(score_kernel, grid=(total // step,), in_specs=[pl.BlockSpe...  18.7 us
    pallas_call x1, Pallas kernels, merge(): pl.pallas_call(kernel, grid=(halves * per,), in_specs=[pl.BlockSpec((step...  10.7 us
    pallas_call x1, Pallas kernels, enqueue(): pl.pallas_call(kernel, grid=(slots // step,), in_specs=[pl.BlockSpec(memo...  6.99 us
    pallas_call x1, Pallas kernels, pack(): pl.pallas_call(pack_kernel, grid=(shards // 16,), in_specs=[pl.BlockSpec(...  6.55 us
  transfers between devices with their start and end apart: 3, of which 1 were waited for; matrix products, arithmetic and copies ran while one was open for 0% of the time, Pallas kernels for 14%

profile of v1, /device:TPU:1, one launch (start us, length us, event | category | flops | bytes accessed | tf_op | source)
XLA Modules:
  0.0 232.0 jit_solution(13458028343819460500)
XLA Ops:
  0.6 1.4 copy.16.pairs_ref
  2.0 6.6 %pack.1 = (bf16[2048,1024]{1,0:T(8,128)(2,1)}, f32[128,128]{1,0:T(8,128)}) custom-call(s32[18,3]{1,0:T(8,128)} %copy.16.pairs_ref, s32[1,144]{1,0:T(1,128)} %bitcast.30, bf16[144,1024]{1,0:T(8,128)(2,1)} %query_ref.3), custom_call_target="tpu_custom_call" | custom-call | tf_op jit(solution)/shard_map/pack/pallas_call | solution.py:66
  8.5 21.3 %all_to_all.25 = f32[128,1,128]{2,1,0:T(1,128)} all-to-all(f32[128,1,128]{2,1,0:T(1,128)} %bitcast.29), channel_id=1, replica_groups=mesh['mem'=64,'grp'=2] {'mem','grp'}, dimensions={0} | all-to-all | bytes 131072 | tf_op jit(solution)/shard_map/all_to_all | solution.py:378
  29.8 58.6 %all_to_all.26 = bf16[128,16,1024]{2,1,0:T(8,128)(2,1)} all-to-all(bf16[128,16,1024]{2,1,0:T(8,128)(2,1)} %bitcast.20), channel_id=1, replica_groups=mesh['mem'=64,'grp'=2] {'mem','grp'}, dimensions={0} | all-to-all | bytes 8388608 | tf_op jit(solution)/shard_map/all_to_all | solution.py:378
  88.4 18.7 %score.1 = (bf16[2048,2048]{1,0:T(8,128)(2,1)}, f32[128,128]{1,0:T(8,128)}) custom-call(bf16[2048,1024]{1,0:T(8,128)(2,1)} %bitcast.21, f32[128,128]{1,0:T(8,128)} %bitcast.24, bf16[2048,1024]{1,0:T(8,128)(2,1)} %refs_2_.1, s32[1,2048]{1,0:T(1,128)} %bitcast.31), custom_call_target="tpu_custom_call" | custom-call | flops 8589934592 | bytes 16777216 | tf_op jit(solution)/shard_map/score/pallas_call | solution.py:111
  107.1 4.3 %all-to-all-start.2 = ((f32[128,1,128]{2,1,0:T(1,128)}), f32[128,1,128]{2,1,0:T(1,128)S(1)}, u32[]{:S(2)}, u32[]{:S(2)}) async-start(f32[128,1,128]{2,1,0:T(1,128)} %bitcast.28), calls=%async_computation.2 | async-start | bytes 131072 | tf_op jit(solution)/shard_map/all_to_all | solution.py:378
  111.4 13.0 %sums.3 = (f32[1024,1024]{1,0:T(8,128)}, f32[1024,1024]{1,0:T(8,128)}) custom-call(bf16[2048,2048]{1,0:T(8,128)(2,1)} %get-tuple-element.20.weight_ref, f32[128,128]{1,0:T(8,128)} %bitcast.25, bf16[2048,1024]{1,0:T(8,128)(2,1)} %refs_2_.1, s32[1,2048]{1,0:T(1,128)} %bitcast.32), custom_call_target="tpu_custom_call" | custom-call | flops 8589934592 | bytes 16777216 | tf_op jit(solution)/shard_map/sums/pallas_call | solution.py:151
  124.4 0.0 all-to-all-done.2
  124.4 0.0 copy-start.1
  124.4 0.6 copy-done.1
  125.0 3.9 %totals.1 = (f32[1,144]{1,0:T(1,128)}, f32[144,1]{1,0:T(8,128)}, f32[128,128]{1,0:T(8,128)}) custom-call(s32[18,3]{1,0:T(8,128)} %copy.16.pairs_ref, bf16[144,1024]{1,0:T(8,128)(2,1)} %query_ref.3, bf16[144,1024]{1,0:T(8,128)(2,1)} %refs_1_.1, f32[128,128]{1,0:T(8,128)} %bitcast.23), custom_call_target="tpu_custom_call" | custom-call | tf_op jit(solution)/shard_map/totals/pallas_call | solution.py:241
  128.9 9.9 %all-to-all-start.3 = ((f32[128,1,128]{2,1,0:T(1,128)}), f32[128,1,128]{2,1,0:T(1,128)S(1)}, u32[]{:S(2)}, u32[]{:S(2)}) async-start(f32[128,1,128]{2,1,0:T(1,128)} %bitcast.27), calls=%async_computation.3 | async-start | bytes 131072 | tf_op jit(solution)/shard_map/all_to_all | solution.py:378
  138.8 13.0 %sums.2 = (f32[1024,1024]{1,0:T(8,128)}, f32[1024,1024]{1,0:T(8,128)}) custom-call(bf16[2048,2048]{1,0:T(8,128)(2,1)} %get-tuple-element.20.weight_ref, f32[128,128]{1,0:T(8,128)} %bitcast.26, bf16[2048,1024]{1,0:T(8,128)(2,1)} %refs_2_.1, s32[1,2048]{1,0:T(1,128)} %bitcast.33), custom_call_target="tpu_custom_call" | custom-call | flops 8589934592 | bytes 16777216 | tf_op jit(solution)/shard_map/sums/pallas_call | solution.py:151
  151.7 0.0 all-to-all-done.3
  151.7 0.0 copy-start
  151.8 0.6 copy-done
  152.4 10.7 %merge.1 = bf16[2048,1024]{1,0:T(8,128)(2,1)} custom-call(f32[128,128]{1,0:T(8,128)} %bitcast.22, f32[1024,1024]{1,0:T(8,128)} %get-tuple-element.21.refs_1_, f32[1024,1024]{1,0:T(8,128)} %get-tuple-element.22.refs_2_, f32[1024,1024]{1,0:T(8,128)} %get-tuple-element.23.refs_3_, f32[1024,1024]{1,0:T(8,128)} %get-tuple-element.24.refs_4_), custom_call_target="tpu_custom_call" | custom-call | tf_op jit(solution)/shard_map/merge/pallas_call | solution.py:283
  163.1 10.2 %all-to-all-start.4 = ((bf16[128,16,1024]{2,1,0:T(8,128)(2,1)}), bf16[128,16,1024]{2,1,0:T(8,128)(2,1)}, u32[]{:S(2)}, u32[]{:S(2)}) async-start(bf16[128,16,1024]{2,1,0:T(8,128)(2,1)} %bitcast.19), calls=%async_computation.4 | async-start | bytes 8388608 | tf_op jit(solution)/shard_map/all_to_all | solution.py:378
  174.0 7.0 %enqueue.1 = bf16[2048,1024]{1,0:T(8,128)(2,1)} custom-call(s32[1]{0:T(128)S(6)} %copy.19.refs_0_, bf16[144,1024]{1,0:T(8,128)(2,1)} %refs_1_.1, bf16[2048,1024]{1,0:T(8,128)(2,1)} %refs_2_.1), custom_call_target="tpu_custom_call" | custom-call | tf_op jit(solution)/shard_map/enqueue/pallas_call | solution.py:360
  181.0 45.0 %all-to-all-done.4 = bf16[128,16,1024]{2,1,0:T(8,128)(2,1)} async-done(((bf16[128,16,1024]{2,1,0:T(8,128)(2,1)}), bf16[128,16,1024]{2,1,0:T(8,128)(2,1)}, u32[]{:S(2)}, u32[]{:S(2)}) %all-to-all-start.4) | async-done | bytes 4194336 | tf_op jit(solution)/shard_map/all_to_all | solution.py:378
  226.0 6.0 %gradient.1 = f32[144,1024]{1,0:T(8,128)} custom-call(s32[18,3]{1,0:T(8,128)} %copy.16.pairs_ref, f32[144,1]{1,0:T(8,128)} %get-tuple-element.18.factor_ref, bf16[144,1024]{1,0:T(8,128)(2,1)} %refs_1_.1, bf16[2048,1024]{1,0:T(8,128)(2,1)} %bitcast.15.back_ref), custom_call_target="tpu_custom_call" | custom-call | tf_op jit(solution)/shard_map/gradient/pallas_call | solution.py:321
Async XLA Ops:
  107.1 17.3 %all-to-all-start.2 = ((f32[128,1,128]{2,1,0:T(1,128)}), f32[128,1,128]{2,1,0:T(1,128)S(1)}, u32[]{:S(2)}, u32[]{:S(2)}) async-start(f32[128,1,128]{2,1,0:T(1,128)} %bitcast.28), calls=%async_computation.2 | async-start | bytes 131072 | tf_op jit(solution)/shard_map/all_to_all | solution.py:378
  124.4 0.6 copy-start.1
  128.9 22.9 %all-to-all-start.3 = ((f32[128,1,128]{2,1,0:T(1,128)}), f32[128,1,128]{2,1,0:T(1,128)S(1)}, u32[]{:S(2)}, u32[]{:S(2)}) async-start(f32[128,1,128]{2,1,0:T(1,128)} %bitcast.27), calls=%async_computation.3 | async-start | bytes 131072 | tf_op jit(solution)/shard_map/all_to_all | solution.py:378
  151.7 0.6 copy-start
  163.1 62.9 %all-to-all-start.4 = ((bf16[128,16,1024]{2,1,0:T(8,128)(2,1)}), bf16[128,16,1024]{2,1,0:T(8,128)(2,1)}, u32[]{:S(2)}, u32[]{:S(2)}) async-start(bf16[128,16,1024]{2,1,0:T(8,128)(2,1)} %bitcast.19), calls=%async_computation.4 | async-start | bytes 8388608 | tf_op jit(solution)/shard_map/all_to_all | solution.py:378

commit v2 on v1

v2 whole, which is shorter than its diff:
```python
import jax
import jax.numpy as jnp
from jax import lax
from jax.experimental import pallas as pl
from jax.experimental.pallas import tpu as pltpu
from jax.sharding import PartitionSpec as P

CAP = 2
F32 = jnp.float32
BF16 = jnp.bfloat16
I32 = jnp.int32
AXES = ("mem", "grp")
LANES = 128
MIB = 1024 * 1024
OWNER_STEP = 512
OWNER_SUB = 256
OWNER_MIB = 26
MERGE_STEP = 512
MERGE_MIB = 16
EXACT = lax.Precision.HIGHEST


def iota(shape, axis):
    return lax.broadcasted_iota(I32, shape, axis)


def targets(pairs_ref, k, block_of):
    out = jnp.zeros(block_of.shape, I32)
    for b in range(pairs_ref.shape[1]):
        out = jnp.where(block_of == b, pairs_ref[k, b], out)
    return out


def spread(packed, rows):
    n = packed.shape[0]
    return jnp.broadcast_to(packed[:, None, :], (n, 16, LANES)).reshape(rows, LANES)


def column_of(wide, group):
    rows = wide.shape[0]
    pick = iota((rows, LANES), 1) == group * 16 + (iota((rows, LANES), 0) & 15)
    return jnp.sum(jnp.where(pick, wide, 0.0), axis=1, keepdims=True)


def pack_kernel(pairs_ref, label_ref, query_ref, send_ref, rows_ref, table_ref):
    step = pl.program_id(0)
    fanout, blocks = pairs_ref.shape
    rows_dev, width = query_ref.shape
    shards = table_ref.shape[0] // CAP

    @pl.when(step == 0)
    def _():
        rows_ref[0:rows_dev, 0:width] = query_ref[...].astype(F32)
        side = (rows_dev, rows_dev)
        label = jnp.where(iota(side, 0) == iota(side, 1), label_ref[...].astype(F32), 0.0)
        label = jnp.sum(label, axis=1, keepdims=True)
        rows_ref[0:rows_dev, width:] = jnp.broadcast_to(label, (rows_dev, LANES))
        rows_ref[rows_dev:, :] = jnp.zeros((8, width + LANES), F32)

        def clear(i, carry):
            table_ref[i] = blocks
            return carry

        lax.fori_loop(0, shards * CAP, clear, 0)

        def enter(b, carry):
            for k in range(fanout):
                at = pairs_ref[k, b] * CAP
                at = at + jnp.where(table_ref[at] == blocks, 0, 1)
                table_ref[at] = b
            return carry

        lax.fori_loop(0, blocks, enter, 0)

    for j in range(send_ref.shape[0] // 16):
        at = (step * (send_ref.shape[0] // 16) + j) * CAP
        pair = [rows_ref[pl.ds(pl.multiple_of(table_ref[at + s] * 8, 8), 8), :] for s in range(CAP)]
        send_ref[j * 16 : (j + 1) * 16, :] = jnp.concatenate(pair, axis=0).astype(BF16)


def pack(pairs, labels, queries, shards):
    rows_dev, width = queries.shape
    step = 512
    return pl.pallas_call(
        pack_kernel,
        grid=(shards * 16 // step,),
        in_specs=[
            pl.BlockSpec(memory_space=pltpu.SMEM),
            pl.BlockSpec((1, rows_dev), lambda i: (0, 0)),
            pl.BlockSpec((rows_dev, width), lambda i: (0, 0)),
        ],
        out_specs=pl.BlockSpec((step, width + LANES), lambda i: (i, 0)),
        out_shape=jax.ShapeDtypeStruct((shards * 16, width + LANES), BF16),
        scratch_shapes=[
            pltpu.VMEM((rows_dev + 8, width + LANES), F32),
            pltpu.SMEM((shards * CAP,), I32),
        ],
        compiler_params=pltpu.CompilerParams(vmem_limit_bytes=16 * MIB),
        name="pack",
    )(pairs, labels.reshape(1, rows_dev), queries)


def owner_kernel(query_ref, memory_ref, slot_label_ref, all_ref, pos_ref, stat_ref):
    width = memory_ref.shape[1]
    sub = OWNER_SUB
    for c in range(query_ref.shape[0] // sub):
        at = slice(c * sub, (c + 1) * sub)
        scores = lax.dot_general(
            query_ref[at, 0:width], memory_ref[...], (((1,), (1,)), ((), ())), preferred_element_type=F32
        )
        top = jnp.max(scores, axis=1, keepdims=True)
        weights = jnp.exp(scores - top)
        row_label = query_ref[at, width : width + LANES].astype(F32)[:, 0:1]
        same = row_label == slot_label_ref[...].astype(F32)
        positive = jnp.where(same, weights, 0.0)
        part_all = jnp.sum(weights, axis=1, keepdims=True)
        part_pos = jnp.sum(positive, axis=1, keepdims=True)
        lane = iota((sub, LANES), 1)
        place = iota((sub, LANES), 0) & 15
        wide = jnp.where(lane == place, top, 0.0)
        wide = jnp.where(lane == place + 16, part_all, wide)
        wide = jnp.where(lane == place + 32, part_pos, wide)
        stat_ref[c * sub // 16 : (c + 1) * sub // 16, :] = jnp.sum(
            wide.reshape(sub // 16, 16, LANES), axis=1
        )
        both = jnp.dot(
            jnp.concatenate([weights.astype(BF16), positive.astype(BF16)], axis=0),
            memory_ref[...],
            preferred_element_type=F32,
        )
        all_ref[at, :] = both[:sub]
        pos_ref[at, :] = both[sub:]


def owner(rows_query, memory, slot_label):
    total = rows_query.shape[0]
    slots, width = memory.shape
    step = OWNER_STEP
    return pl.pallas_call(
        owner_kernel,
        grid=(total // step,),
        in_specs=[
            pl.BlockSpec((step, width + LANES), lambda i: (i, 0)),
            pl.BlockSpec((slots, width), lambda i: (0, 0), pipeline_mode=pl.Buffered(1)),
            pl.BlockSpec((1, slots), lambda i: (0, 0)),
        ],
        out_specs=[
            pl.BlockSpec((step, width), lambda i: (i, 0)),
            pl.BlockSpec((step, width), lambda i: (i, 0)),
            pl.BlockSpec((step // 16, LANES), lambda i: (i, 0)),
        ],
        out_shape=[
            jax.ShapeDtypeStruct((total, width), F32),
            jax.ShapeDtypeStruct((total, width), F32),
            jax.ShapeDtypeStruct((total // 16, LANES), F32),
        ],
        compiler_params=pltpu.CompilerParams(vmem_limit_bytes=OWNER_MIB * MIB),
        cost_estimate=pl.CostEstimate(
            flops=6 * total * slots * width, bytes_accessed=24 * MIB, transcendentals=total * slots
        ),
        name="owner",
    )(rows_query, memory, slot_label)


def total_kernel(pairs_ref, query_ref, key_ref, stat_ref, loss_ref, factor_ref, back_ref):
    rows = query_ref.shape[0]
    fanout = pairs_ref.shape[0]
    own = jnp.sum(query_ref[...].astype(F32) * key_ref[...].astype(F32), axis=1, keepdims=True)
    stat = stat_ref[...]
    stat_slot = (iota(stat.shape, 1) >> 3) & 1

    down_block = iota((rows, 1), 0) >> 3
    down_match = [
        (targets(pairs_ref, k, down_block) == iota((rows, LANES), 1)).astype(F32) for k in range(fanout)
    ]
    side = (rows, rows)
    earlier_down = ((iota(side, 1) >> 3) < (iota(side, 0) >> 3)) & ((iota(side, 1) & 7) == 0)
    down_count = jnp.dot(
        earlier_down.astype(F32).astype(BF16),
        sum(down_match[1:], down_match[0]).astype(BF16),
        preferred_element_type=F32,
    )
    lane = iota((rows, LANES), 1)
    mine = (lane & 7) == (iota((rows, LANES), 0) & 7)
    maxima, alls, poss = [], [], []
    for k in range(fanout):
        wide = jnp.zeros((rows, LANES), F32)
        for s in range(CAP):
            mask = jnp.where(down_count == s, down_match[k], 0.0)
            wide = wide + jnp.dot(
                mask, jnp.where(stat_slot == s, stat, 0.0), precision=EXACT, preferred_element_type=F32
            )
        for group, into in enumerate((maxima, alls, poss)):
            pick = mine & ((lane >> 4) == group)
            into.append(jnp.sum(jnp.where(pick, wide, 0.0), axis=1, keepdims=True))
    top = own
    for value in maxima:
        top = jnp.maximum(top, value)
    own_weight = jnp.exp(own - top)
    scales = [jnp.exp(value - top) for value in maxima]
    total_all, total_pos = own_weight, own_weight
    for k in range(fanout):
        total_all = total_all + scales[k] * alls[k]
        total_pos = total_pos + scales[k] * poss[k]
    loss = jnp.log(total_all) - jnp.log(total_pos)
    loss_ref[...] = jnp.sum(jnp.where(iota(side, 0) == iota(side, 1), loss, 0.0), axis=0, keepdims=True)
    factor_ref[...] = own_weight * (1.0 / total_all - 1.0 / total_pos)

    across_block = iota((1, rows), 1) >> 3
    across_match = [
        (targets(pairs_ref, k, across_block) == iota((LANES, rows), 0)).astype(F32) for k in range(fanout)
    ]
    earlier_across = ((iota(side, 0) >> 3) < (iota(side, 1) >> 3)) & ((iota(side, 0) & 7) == 0)
    across_count = jnp.dot(
        sum(across_match[1:], across_match[0]).astype(BF16),
        earlier_across.astype(F32).astype(BF16),
        preferred_element_type=F32,
    )
    back = jnp.zeros((LANES, LANES), F32)
    for k in range(fanout):
        factor_all, factor_pos = scales[k] / total_all, scales[k] / total_pos
        for s in range(CAP):
            mask = jnp.where(across_count == s, across_match[k], 0.0)
            value = jnp.where((lane >> 3) == s, factor_all, 0.0)
            value = jnp.where((lane >> 3) == 2 + s, factor_pos, value)
            value = jnp.where(mine, value, 0.0)
            back = back + jnp.dot(mask, value, precision=EXACT, preferred_element_type=F32)
    back_ref[...] = back


def totals(pairs, queries, keys, stat):
    rows = queries.shape[0]
    return pl.pallas_call(
        total_kernel,
        in_specs=[pl.BlockSpec(memory_space=pltpu.SMEM)] + [pl.BlockSpec(memory_space=pltpu.VMEM)] * 3,
        out_specs=[pl.BlockSpec(memory_space=pltpu.VMEM)] * 3,
        out_shape=[
            jax.ShapeDtypeStruct((1, rows), F32),
            jax.ShapeDtypeStruct((rows, 1), F32),
            jax.ShapeDtypeStruct(stat.shape, F32),
        ],
        compiler_params=pltpu.CompilerParams(vmem_limit_bytes=16 * MIB),
        name="totals",
    )(pairs, queries, keys, stat)


def merge_kernel(factor_ref, all_ref, pos_ref, out_ref):
    wide = spread(factor_ref[...], out_ref.shape[0])
    factor_all, factor_pos = column_of(wide, 0), column_of(wide, 1)
    out_ref[...] = (factor_all * all_ref[...] - factor_pos * pos_ref[...]).astype(BF16)


def merge(factors, sum_all, sum_pos):
    total, width = sum_all.shape
    step = MERGE_STEP
    return pl.pallas_call(
        merge_kernel,
        grid=(total // step,),
        in_specs=[pl.BlockSpec((step // 16, LANES), lambda i: (i, 0))]
        + [pl.BlockSpec((step, width), lambda i: (i, 0))] * 2,
        out_specs=pl.BlockSpec((step, width), lambda i: (i, 0)),
        out_shape=pltpu.HBM((total, width), BF16),
        compiler_params=pltpu.CompilerParams(vmem_limit_bytes=MERGE_MIB * MIB),
        name="merge",
    )(factors, sum_all, sum_pos)


def picker_kernel(pairs_ref, out_ref):
    rows, total = out_ref.shape
    block = iota((rows, 1), 0) >> 3
    place = iota((rows, total), 1)
    match = jnp.zeros((rows, total), F32)
    for k in range(pairs_ref.shape[0]):
        match = jnp.where(targets(pairs_ref, k, block) == (place >> 4), 1.0, match)
    side = (rows, rows)
    earlier = ((iota(side, 1) >> 3) < (iota(side, 0) >> 3)) & ((iota(side, 1) & 7) == 0)
    count = jnp.dot(earlier.astype(F32).astype(BF16), match.astype(BF16), preferred_element_type=F32)
    chosen = jnp.where(count == ((place >> 3) & 1).astype(F32), match, 0.0)
    chosen = jnp.where((place & 7) == (iota((rows, total), 0) & 7), chosen, 0.0)
    out_ref[...] = chosen.astype(BF16)


def picker(pairs, rows, total):
    return pl.pallas_call(
        picker_kernel,
        in_specs=[pl.BlockSpec(memory_space=pltpu.SMEM)],
        out_specs=pl.BlockSpec(memory_space=pltpu.VMEM),
        out_shape=jax.ShapeDtypeStruct((rows, total), BF16),
        compiler_params=pltpu.CompilerParams(vmem_limit_bytes=16 * MIB),
        name="picker",
    )(pairs)


def enqueue_kernel(slots, offset_ref, key_ref, memory_ref, out_ref):
    rows = memory_ref.shape[0]
    count = key_ref.shape[0]
    distance = iota((rows, 1), 0) + (pl.program_id(0) * rows - offset_ref[0] + slots)
    distance = jnp.where(distance >= slots, distance - slots, distance)
    lead = lax.rem(pl.program_id(0) * rows - offset_ref[0] + slots, slots)
    out_ref[...] = memory_ref[...]

    @pl.when((lead < count) | (lead + rows > slots))
    def _():
        pick = (distance == iota((rows, count), 1)).astype(F32).astype(BF16)
        fresh = jnp.dot(pick, key_ref[...], preferred_element_type=F32)
        out_ref[...] = jnp.where(distance < count, fresh, memory_ref[...].astype(F32)).astype(BF16)


def enqueue(offset, keys, memory):
    slots, width = memory.shape
    count = keys.shape[0]
    step = 512

    def kernel(*refs):
        enqueue_kernel(slots, *refs)

    return pl.pallas_call(
        kernel,
        grid=(slots // step,),
        in_specs=[
            pl.BlockSpec(memory_space=pltpu.SMEM),
            pl.BlockSpec((count, width), lambda i: (0, 0)),
            pl.BlockSpec((step, width), lambda i: (i, 0)),
        ],
        out_specs=pl.BlockSpec((step, width), lambda i: (i, 0)),
        out_shape=jax.ShapeDtypeStruct((slots, width), BF16),
        compiler_params=pltpu.CompilerParams(vmem_limit_bytes=24 * MIB),
        name="enqueue",
    )(offset, keys, memory)


def exchange(rows, per):
    shards = lax.axis_size(AXES)
    grouped = rows.reshape(shards, per, rows.shape[1])
    moved = lax.all_to_all(grouped, AXES, split_axis=0, concat_axis=0, tiled=True)
    return moved.reshape(rows.shape)


def body(queries, keys, labels, memory, mem_labels, pairs, offset):
    shards = lax.axis_size(AXES)
    rows_dev, width = queries.shape
    slots = memory.shape[0]
    slot_label = mem_labels.reshape(1, slots)
    pairs = pairs.T
    rows_query = exchange(pack(pairs, labels, queries, shards), 16)
    sum_all, sum_pos, stat = owner(rows_query, memory, slot_label)
    loss, factor, factors = totals(pairs, queries, keys, exchange(stat, 1))
    back = merge(exchange(factors, 1), sum_all, sum_pos)
    back, held, pairs = lax.optimization_barrier((back, memory, pairs))
    back = exchange(back, 16)
    updated = enqueue(offset, keys, held)
    picked = picker(pairs, rows_dev, shards * 16)
    grad = jnp.dot(picked, back, preferred_element_type=F32) + factor * keys.astype(F32)
    return loss.reshape(rows_dev), grad, updated


def solution(mesh):
    in_specs = (
        P(AXES, None),
        P(AXES, None),
        P(AXES),
        P(AXES, None),
        P(AXES),
        P(AXES, None),
        P(),
    )
    out_specs = (P(AXES), P(AXES, None), P(AXES, None))
    return jax.shard_map(body, mesh=mesh, in_specs=in_specs, out_specs=out_specs, check_vma=False)
```

time: 233 us -> 203 us (0.87)
  Pallas kernels: 78.7 us -> 44.2 us
  starting transfers between devices: 24.4 us -> 5.31 us
  blocking collectives: 79.9 us -> 97.8 us
  matrix products: 0 us -> 3.8 us
    pallas_call x6 -> x4, Pallas kernels: 67.9 us -> 38.6 us  [the longest x1 30.7 us: owner(): pl.pallas_call(owner_kernel, grid=(total // step,), in_specs=[pl.BlockSpe...]
    all_to_all x3 -> x1, starting transfers between devices: 24.4 us -> 5.31 us  [exchange(): lax.all_to_all(grouped, AXES, split_axis=0, concat_axis=0, tiled=True)]
    all_to_all x2 -> x3, blocking collectives: 79.9 us -> 97.8 us  [exchange(): lax.all_to_all(grouped, AXES, split_axis=0, concat_axis=0, tiled=True)]
    pallas_call x1, Pallas kernels: 6.99 us -> 2.9 us  [enqueue(): pl.pallas_call(kernel, grid=(slots // step,), in_specs=[pl.BlockSpec(memo...]
    dot_general x0 -> x1, matrix products: none -> 3.8 us  [body(): jnp.dot(picked, back, preferred_element_type=F32)]
    all_to_all x3 -> x1, waiting for transfers between devices: 45 us -> 45.6 us  [exchange(): lax.all_to_all(grouped, AXES, split_axis=0, concat_axis=0, tiled=True)]
  transfers between devices with their start and end apart: 3 -> 1, of which waited for: 1 -> 1; matrix products, arithmetic and copies ran while one was open for 0% -> 0% of each run, Pallas kernels for 14% -> 2%
where the time goes in v2:
time: 203 us
  blocking collectives  97.8 us (48%)
  waiting for transfers between devices  45.6 us (22%)
  Pallas kernels  44.2 us (22%)
  starting transfers between devices  5.31 us (3%)
  local copies, waits for them, and re-layouts  4.53 us (2%)
  matrix products  3.8 us (2%)
    all_to_all x3, blocking collectives, exchange(): lax.all_to_all(grouped, AXES, split_axis=0, concat_axis=0, tiled=True)  97.8 us
    all_to_all x1, waiting for transfers between devices, exchange(): lax.all_to_all(grouped, AXES, split_axis=0, concat_axis=0, tiled=True)  45.6 us
    pallas_call x1, Pallas kernels, owner(): pl.pallas_call(owner_kernel, grid=(total // step,), in_specs=[pl.BlockSpe...  30.7 us
    all_to_all x1, starting transfers between devices, exchange(): lax.all_to_all(grouped, AXES, split_axis=0, concat_axis=0, tiled=True)  5.31 us
    unnamed x18, local copies, waits for them, and re-layouts  4.53 us
  transfers between devices with their start and end apart: 1, of which 1 were waited for; matrix products, arithmetic and copies ran while one was open for 0% of the time, Pallas kernels for 2%

profile of v2, /device:TPU:1, one launch (start us, length us, event | category | flops | bytes accessed | tf_op | source)
XLA Modules:
  0.0 202.8 jit_solution(15309253182711179944)
XLA Ops:
  0.6 0.0 copy-start.3
  0.6 1.0 copy-done.3
  1.6 0.0 copy-start.5
  1.6 0.7 copy-done.5
  2.3 0.0 copy-start.7
  2.3 0.7 copy-done.7
  3.0 3.4 %pack.1 = bf16[2048,1152]{1,0:T(8,128)(2,1)S(1)} custom-call(s32[3,18]{1,0:T(4,128)S(1)} %bitcast.24, s32[1,144]{1,0:T(1,128)S(1)} %bitcast.27, bf16[144,1024]{1,0:T(8,128)(2,1)S(1)} %copy-done.3), custom_call_target="tpu_custom_call" | custom-call | tf_op jit(solution)/shard_map/pack/pallas_call | solution.py:84
  6.3 0.0 copy-start
  6.3 0.0 copy-start.8
  6.3 70.0 %all_to_all.20 = bf16[128,16,1152]{2,1,0:T(8,128)(2,1)S(1)} all-to-all(bf16[128,16,1152]{2,1,0:T(8,128)(2,1)S(1)} %bitcast.18), channel_id=1, replica_groups=mesh['mem'=64,'grp'=2] {'mem','grp'}, dimensions={0} | all-to-all | bytes 9437184 | tf_op jit(solution)/shard_map/all_to_all | solution.py:335
  76.3 0.0 copy-done
  76.3 0.0 copy-done.8
  76.3 0.0 copy-start.2
  76.3 0.0 copy-start.4
  76.3 0.0 copy-start.6
  76.3 30.7 %owner.1 = (f32[2048,1024]{1,0:T(8,128)S(1)}, f32[2048,1024]{1,0:T(8,128)S(1)}, f32[128,128]{1,0:T(8,128)S(1)}) custom-call(bf16[2048,1152]{1,0:T(8,128)(2,1)S(1)} %bitcast.19, bf16[2048,1024]{1,0:T(8,128)(2,1)S(1)} %copy-done, s32[1,2048]{1,0:T(1,128)S(1)} %bitcast.28), custom_call_target="tpu_custom_call" | custom-call | flops 25769803776 | bytes 25165824 | tf_op jit(solution)/shard_map/owner/pallas_call | solution.py:139
  107.0 13.9 %all_to_all.21 = f32[128,1,128]{2,1,0:T(1,128)S(1)} all-to-all(f32[128,1,128]{2,1,0:T(1,128)S(1)} %bitcast.22), channel_id=1, replica_groups=mesh['mem'=64,'grp'=2] {'mem','grp'}, dimensions={0} | all-to-all | bytes 131072 | tf_op jit(solution)/shard_map/all_to_all | solution.py:335
  120.9 0.0 copy-done.2
  121.0 0.0 copy-done.4
  121.0 0.0 copy-done.6
  121.0 2.7 %totals.1 = (f32[1,144]{1,0:T(1,128)}, f32[144,1]{1,0:T(8,128)S(1)}, f32[128,128]{1,0:T(8,128)S(1)}) custom-call(s32[3,18]{1,0:T(4,128)S(1)} %bitcast.25, bf16[144,1024]{1,0:T(8,128)(2,1)S(1)} %copy-done.4, bf16[144,1024]{1,0:T(8,128)(2,1)S(1)} %copy-done.2, f32[128,128]{1,0:T(8,128)S(1)} %bitcast.21), custom_call_target="tpu_custom_call" | custom-call | tf_op jit(solution)/shard_map/totals/pallas_call | solution.py:233
  123.7 13.9 %all_to_all.22 = f32[128,1,128]{2,1,0:T(1,128)S(1)} all-to-all(f32[128,1,128]{2,1,0:T(1,128)S(1)} %bitcast.23), channel_id=1, replica_groups=mesh['mem'=64,'grp'=2] {'mem','grp'}, dimensions={0} | all-to-all | bytes 131072 | tf_op jit(solution)/shard_map/all_to_all | solution.py:335
  137.6 3.2 %merge.1 = bf16[2048,1024]{1,0:T(8,128)(2,1)} custom-call(f32[128,128]{1,0:T(8,128)S(1)} %bitcast.20, f32[2048,1024]{1,0:T(8,128)S(1)} %get-tuple-element.15.all_ref, f32[2048,1024]{1,0:T(8,128)S(1)} %get-tuple-element.16.pos_ref), custom_call_target="tpu_custom_call" | custom-call | tf_op jit(solution)/shard_map/merge/pallas_call | solution.py:256
  140.9 5.3 %all-to-all-start.3 = ((bf16[128,16,1024]{2,1,0:T(8,128)(2,1)}), bf16[128,16,1024]{2,1,0:T(8,128)(2,1)}, u32[]{:S(2)}, u32[]{:S(2)}) async-start(bf16[128,16,1024]{2,1,0:T(8,128)(2,1)} %bitcast.29), calls=%async_computation.3 | async-start | bytes 8388608 | tf_op jit(solution)/shard_map/all_to_all | solution.py:335
  146.8 0.1 reduce
  146.9 1.3 picker.1
  148.3 0.0 copy-start.1
  148.3 2.2 %copy-done.1 = bf16[2048,1024]{1,0:T(8,128)(2,1)S(1)} copy-done((bf16[2048,1024]{1,0:T(8,128)(2,1)S(1)}, bf16[2048,1024]{1,0:T(8,128)(2,1)}, u32[]{:S(2)}) %copy-start.1) | copy-done | bytes 4194328
  150.4 2.9 %enqueue.1 = bf16[2048,1024]{1,0:T(8,128)(2,1)} custom-call(s32[1]{0:T(128)S(6)} %copy.12.refs_0_, bf16[144,1024]{1,0:T(8,128)(2,1)S(1)} %copy-done.2, bf16[2048,1024]{1,0:T(8,128)(2,1)S(1)} %copy-done.1), custom_call_target="tpu_custom_call" | custom-call | tf_op jit(solution)/shard_map/enqueue/pallas_call | solution.py:317
  153.3 45.6 %all-to-all-done.3 = bf16[128,16,1024]{2,1,0:T(8,128)(2,1)} async-done(((bf16[128,16,1024]{2,1,0:T(8,128)(2,1)}), bf16[128,16,1024]{2,1,0:T(8,128)(2,1)}, u32[]{:S(2)}, u32[]{:S(2)}) %all-to-all-start.3) | async-done | bytes 4194336 | tf_op jit(solution)/shard_map/all_to_all | solution.py:335
  199.0 3.8 %convolution_add_fusion = f32[144,1024]{1,0:T(8,128)} fusion(bf16[144,2048]{1,0:T(8,128)(2,1)S(1)} %picker.1, bf16[2048,1024]{1,0:T(8,128)(2,1)} %bitcast.13, bf16[144,1024]{1,0:T(8,128)(2,1)S(1)} %copy-done.2, f32[144]{0:T(256)S(1)} %reduce), kind=kOutput, calls=%fused_computation | convolution fusion | flops 604422144 | bytes 5669440 | tf_op jit(solution)/shard_map/dot_general | solution.py:353
Async XLA Ops:
  0.6 1.0 copy-start.3
  1.6 0.7 copy-start.5
  2.3 0.7 copy-start.7
  6.3 70.0 %copy-start = (bf16[2048,1024]{1,0:T(8,128)(2,1)S(1)}, bf16[2048,1024]{1,0:T(8,128)(2,1)}, u32[]{:S(2)}) copy-start(bf16[2048,1024]{1,0:T(8,128)(2,1)} %refs_2_) | copy-start | bytes 12582916
  6.3 70.0 %copy-start.8 = (s32[2048]{0:T(1024)S(1)}, s32[2048]{0:T(1024)}, u32[]{:S(2)}) copy-start(s32[2048]{0:T(1024)} %param.11) | copy-start | bytes 24580
  76.3 44.6 %copy-start.2 = (bf16[144,1024]{1,0:T(8,128)(2,1)S(1)}, bf16[144,1024]{1,0:T(8,128)(2,1)}, u32[]{:S(2)}) copy-start(bf16[144,1024]{1,0:T(8,128)(2,1)} %refs_1_.1) | copy-start | bytes 884740
  76.3 44.6 %copy-start.4 = (bf16[144,1024]{1,0:T(8,128)(2,1)S(1)}, bf16[144,1024]{1,0:T(8,128)(2,1)}, u32[]{:S(2)}) copy-start(bf16[144,1024]{1,0:T(8,128)(2,1)} %query_ref.3) | copy-start | bytes 884740
  76.3 44.6 %copy-start.6 = (s32[18,3]{0,1:T(4,128)S(1)}, s32[18,3]{0,1:T(4,128)}, u32[]{:S(2)}) copy-start(s32[18,3]{0,1:T(4,128)} %param.12) | copy-start | bytes 652
  140.9 58.1 %all-to-all-start.3 = ((bf16[128,16,1024]{2,1,0:T(8,128)(2,1)}), bf16[128,16,1024]{2,1,0:T(8,128)(2,1)}, u32[]{:S(2)}, u32[]{:S(2)}) async-start(bf16[128,16,1024]{2,1,0:T(8,128)(2,1)} %bitcast.29), calls=%async_computation.3 | async-start | bytes 8388608 | tf_op jit(solution)/shard_map/all_to_all | solution.py:335
  148.3 2.2 %copy-start.1 = (bf16[2048,1024]{1,0:T(8,128)(2,1)S(1)}, bf16[2048,1024]{1,0:T(8,128)(2,1)}, u32[]{:S(2)}) copy-start(bf16[2048,1024]{1,0:T(8,128)(2,1)} %refs_2_) | copy-start | bytes 12582916

commit v3 on v2

--- a/solution.py
+++ b/solution.py
@@ -43,74 +43,95 @@
 
 
 def pack_kernel(pairs_ref, label_ref, query_ref, send_ref, rows_ref, table_ref):
-    step = pl.program_id(0)
     fanout, blocks = pairs_ref.shape
     rows_dev, width = query_ref.shape
-    shards = table_ref.shape[0] // CAP
-
-    @pl.when(step == 0)
-    def _():
-        rows_ref[0:rows_dev, 0:width] = query_ref[...].astype(F32)
-        side = (rows_dev, rows_dev)
-        label = jnp.where(iota(side, 0) == iota(side, 1), label_ref[...].astype(F32), 0.0)
-        label = jnp.sum(label, axis=1, keepdims=True)
-        rows_ref[0:rows_dev, width:] = jnp.broadcast_to(label, (rows_dev, LANES))
-        rows_ref[rows_dev:, :] = jnp.zeros((8, width + LANES), F32)
-
-        def clear(i, carry):
-            table_ref[i] = blocks
-            return carry
-
-        lax.fori_loop(0, shards * CAP, clear, 0)
-
-        def enter(b, carry):
-            for k in range(fanout):
-                at = pairs_ref[k, b] * CAP
-                at = at + jnp.where(table_ref[at] == blocks, 0, 1)
-                table_ref[at] = b
-            return carry
-
-        lax.fori_loop(0, blocks, enter, 0)
-
-    for j in range(send_ref.shape[0] // 16):
-        at = (step * (send_ref.shape[0] // 16) + j) * CAP
-        pair = [rows_ref[pl.ds(pl.multiple_of(table_ref[at + s] * 8, 8), 8), :] for s in range(CAP)]
-        send_ref[j * 16 : (j + 1) * 16, :] = jnp.concatenate(pair, axis=0).astype(BF16)
+    shards = send_ref.shape[0]
+    rows_ref[0:rows_dev, 0:width] = query_ref[...].astype(F32)
+    side = (rows_dev, rows_dev)
+    label = jnp.where(iota(side, 0) == iota(side, 1), label_ref[...].astype(F32), 0.0)
+    label = jnp.sum(label, axis=1, keepdims=True)
+    rows_ref[0:rows_dev, width:] = jnp.broadcast_to(label, (rows_dev, LANES))
+    rows_ref[rows_dev:, :] = jnp.zeros((8, width + LANES), F32)
+
+    def clear(i, carry):
+        for u in range(16):
+            table_ref[i * 16 + u] = blocks
+        return carry
+
+    lax.fori_loop(0, shards * CAP // 16, clear, 0)
+
+    def enter(b, carry):
+        for k in range(fanout):
+            at = pairs_ref[k, b] * CAP
+            at = at + jnp.where(table_ref[at] == blocks, 0, 1)
+            table_ref[at] = b
+        return carry
+
+    lax.fori_loop(0, blocks, enter, 0)
+
+    def fill(i, carry):
+        for u in range(4):
+            t = i * 4 + u
+            pair = [
+                rows_ref[pl.ds(pl.multiple_of(table_ref[t * CAP + s] * 8, 8), 8), :] for s in range(CAP)
+            ]
+            both = jnp.concatenate(pair, axis=0)
+            for c in range(width // LANES):
+                send_ref[t, c * 16 : (c + 1) * 16, :] = both[:, c * LANES : (c + 1) * LANES].astype(BF16)
+            first, second = pair[0][:, width:], pair[1][:, width:]
+            label = jnp.where(iota((8, LANES), 1) < LANES // 2, first, second)
+            send_ref[t, width // 8 :, :] = label.astype(BF16)
+        return carry
+
+    lax.fori_loop(0, shards // 4, fill, 0)
+
+
+def in_hbm(array):
+    return pltpu.with_memory_space_constraint(array, pltpu.HBM)
 
 
 def pack(pairs, labels, queries, shards):
     rows_dev, width = queries.shape
-    step = 512
     return pl.pallas_call(
         pack_kernel,
-        grid=(shards * 16 // step,),
         in_specs=[
             pl.BlockSpec(memory_space=pltpu.SMEM),
-            pl.BlockSpec((1, rows_dev), lambda i: (0, 0)),
-            pl.BlockSpec((rows_dev, width), lambda i: (0, 0)),
-        ],
-        out_specs=pl.BlockSpec((step, width + LANES), lambda i: (i, 0)),
-        out_shape=jax.ShapeDtypeStruct((shards * 16, width + LANES), BF16),
+            pl.BlockSpec(memory_space=pltpu.VMEM),
+            pl.BlockSpec(memory_space=pltpu.VMEM),
+        ],
+        out_specs=pl.BlockSpec(memory_space=pltpu.VMEM),
+        out_shape=pltpu.VMEM((shards, width // 8 + 8, LANES), BF16),
         scratch_shapes=[
             pltpu.VMEM((rows_dev + 8, width + LANES), F32),
             pltpu.SMEM((shards * CAP,), I32),
         ],
         compiler_params=pltpu.CompilerParams(vmem_limit_bytes=16 * MIB),
         name="pack",
-    )(pairs, labels.reshape(1, rows_dev), queries)
+    )(in_hbm(pairs), in_hbm(labels.reshape(1, rows_dev)), in_hbm(queries))
 
 
 def owner_kernel(query_ref, memory_ref, slot_label_ref, all_ref, pos_ref, stat_ref):
     width = memory_ref.shape[1]
     sub = OWNER_SUB
-    for c in range(query_ref.shape[0] // sub):
+    for c in range(OWNER_STEP // sub):
         at = slice(c * sub, (c + 1) * sub)
+        places = slice(c * sub // 16, (c + 1) * sub // 16)
+        query = jnp.concatenate(
+            [
+                query_ref[places, i * 16 : (i + 1) * 16, :].reshape(sub, LANES)
+                for i in range(width // LANES)
+            ],
+            axis=1,
+        )
+        label = query_ref[places, width // 8 :, :].astype(F32)
+        half = LANES // 2
+        label = jnp.concatenate([label[:, :, 0:half], label[:, :, half:]], axis=1)
+        row_label = label.reshape(sub, half)[:, 0:1]
         scores = lax.dot_general(
-            query_ref[at, 0:width], memory_ref[...], (((1,), (1,)), ((), ())), preferred_element_type=F32
+            query, memory_ref[...], (((1,), (1,)), ((), ())), preferred_element_type=F32
         )
         top = jnp.max(scores, axis=1, keepdims=True)
         weights = jnp.exp(scores - top)
-        row_label = query_ref[at, width : width + LANES].astype(F32)[:, 0:1]
         same = row_label == slot_label_ref[...].astype(F32)
         positive = jnp.where(same, weights, 0.0)
         part_all = jnp.sum(weights, axis=1, keepdims=True)
@@ -133,14 +154,15 @@
 
 
 def owner(rows_query, memory, slot_label):
-    total = rows_query.shape[0]
+    shards, pieces = rows_query.shape[:2]
+    total = shards * 16
     slots, width = memory.shape
     step = OWNER_STEP
     return pl.pallas_call(
         owner_kernel,
         grid=(total // step,),
         in_specs=[
-            pl.BlockSpec((step, width + LANES), lambda i: (i, 0)),
+            pl.BlockSpec((step // 16, pieces, LANES), lambda i: (i, 0, 0)),
             pl.BlockSpec((slots, width), lambda i: (0, 0), pipeline_mode=pl.Buffered(1)),
             pl.BlockSpec((1, slots), lambda i: (0, 0)),
         ],
@@ -329,11 +351,13 @@
     )(offset, keys, memory)
 
 
+def deal(groups):
+    return lax.all_to_all(groups, AXES, split_axis=0, concat_axis=0, tiled=True)
+
+
 def exchange(rows, per):
     shards = lax.axis_size(AXES)
-    grouped = rows.reshape(shards, per, rows.shape[1])
-    moved = lax.all_to_all(grouped, AXES, split_axis=0, concat_axis=0, tiled=True)
-    return moved.reshape(rows.shape)
+    return deal(rows.reshape(shards, per, rows.shape[1])).reshape(rows.shape)
 
 
 def body(queries, keys, labels, memory, mem_labels, pairs, offset):
@@ -342,7 +366,7 @@
     slots = memory.shape[0]
     slot_label = mem_labels.reshape(1, slots)
     pairs = pairs.T
-    rows_query = exchange(pack(pairs, labels, queries, shards), 16)
+    rows_query = deal(pack(pairs, labels, queries, shards))
     sum_all, sum_pos, stat = owner(rows_query, memory, slot_label)
     loss, factor, factors = totals(pairs, queries, keys, exchange(stat, 1))
     back = merge(exchange(factors, 1), sum_all, sum_pos)

time: 203 us -> 197 us (0.970)
  blocking collectives: 97.8 us -> 95.1 us
  local copies, waits for them, and re-layouts: 4.53 us -> 2.21 us
    all_to_all x3, blocking collectives: 97.8 us -> 95.1 us  [deal(): return lax.all_to_all(groups, AXES, split_axis=0, concat_axis=0, tiled=True)]
    unnamed x18 -> x12, local copies, waits for them, and re-layouts: 4.53 us -> 2.21 us
where the time goes in v3:
time: 197 us
  blocking collectives  95.1 us (48%)
  waiting for transfers between devices  45.6 us (23%)
  Pallas kernels  43.6 us (22%)
  starting transfers between devices  5.3 us (3%)
  matrix products  3.8 us (2%)
  local copies, waits for them, and re-layouts  2.21 us (1%)
    all_to_all x3, blocking collectives, deal(): return lax.all_to_all(groups, AXES, split_axis=0, concat_axis=0, tiled=True)  95.1 us
    all_to_all x1, waiting for transfers between devices, deal(): return lax.all_to_all(groups, AXES, split_axis=0, concat_axis=0, tiled=True)  45.6 us
    pallas_call x1, Pallas kernels, owner(): pl.pallas_call(owner_kernel, grid=(total // step,), in_specs=[pl.BlockSpe...  30.8 us
    all_to_all x1, starting transfers between devices, deal(): return lax.all_to_all(groups, AXES, split_axis=0, concat_axis=0, tiled=True)  5.3 us
  transfers between devices with their start and end apart: 1, of which 1 were waited for; matrix products, arithmetic and copies ran while one was open for 0% of the time, Pallas kernels for 2%

profile of v3, /device:TPU:1, one launch (start us, length us, event | category | flops | bytes accessed | tf_op | source)
XLA Modules:
  0.0 197.1 jit_solution(451468867853859715)
XLA Ops:
  0.6 2.6 %pack.1 = bf16[128,136,128]{2,1,0:T(8,128)(2,1)S(1)} custom-call(s32[3,18]{1,0:T(4,128)} %bitcast.20, s32[1,144]{1,0:T(1,128)} %bitcast.25, bf16[144,1024]{1,0:T(8,128)(2,1)} %query_ref.3), custom_call_target="tpu_custom_call" | custom-call | tf_op jit(solution)/shard_map/pack/pallas_call | solution.py:95
  3.2 0.0 copy-start
  3.2 0.0 copy-start.5
  3.2 67.3 %all_to_all.20.query_ref = bf16[128,136,128]{2,1,0:T(8,128)(2,1)S(1)} all-to-all(bf16[128,136,128]{2,1,0:T(8,128)(2,1)S(1)} %pack.1), channel_id=1, replica_groups=mesh['mem'=64,'grp'=2] {'mem','grp'}, dimensions={0} | all-to-all | bytes 8912896 | tf_op jit(solution)/shard_map/all_to_all | solution.py:355
  70.6 0.0 copy-done
  70.6 0.0 copy-done.5
  70.6 0.0 copy-start.2
  70.6 0.0 copy-start.3
  70.6 0.0 copy-start.4
  70.6 30.8 %owner.1 = (f32[2048,1024]{1,0:T(8,128)S(1)}, f32[2048,1024]{1,0:T(8,128)S(1)}, f32[128,128]{1,0:T(8,128)S(1)}) custom-call(bf16[128,136,128]{2,1,0:T(8,128)(2,1)S(1)} %all_to_all.20.query_ref, bf16[2048,1024]{1,0:T(8,128)(2,1)S(1)} %copy-done, s32[1,2048]{1,0:T(1,128)S(1)} %bitcast.23), custom_call_target="tpu_custom_call" | custom-call | flops 25769803776 | bytes 25165824 | tf_op jit(solution)/shard_map/owner/pallas_call | solution.py:161
  101.4 13.8 %all_to_all.21 = f32[128,1,128]{2,1,0:T(1,128)S(1)} all-to-all(f32[128,1,128]{2,1,0:T(1,128)S(1)} %bitcast.18), channel_id=1, replica_groups=mesh['mem'=64,'grp'=2] {'mem','grp'}, dimensions={0} | all-to-all | bytes 131072 | tf_op jit(solution)/shard_map/all_to_all | solution.py:355
  115.3 0.0 copy-done.2
  115.3 0.0 copy-done.3
  115.3 0.0 copy-done.4
  115.3 2.7 %totals.1 = (f32[1,144]{1,0:T(1,128)}, f32[144,1]{1,0:T(8,128)S(1)}, f32[128,128]{1,0:T(8,128)S(1)}) custom-call(s32[3,18]{1,0:T(4,128)S(1)} %bitcast.21, bf16[144,1024]{1,0:T(8,128)(2,1)S(1)} %copy-done.3, bf16[144,1024]{1,0:T(8,128)(2,1)S(1)} %copy-done.2, f32[128,128]{1,0:T(8,128)S(1)} %bitcast.17), custom_call_target="tpu_custom_call" | custom-call | tf_op jit(solution)/shard_map/totals/pallas_call | solution.py:255
  118.0 13.9 %all_to_all.22 = f32[128,1,128]{2,1,0:T(1,128)S(1)} all-to-all(f32[128,1,128]{2,1,0:T(1,128)S(1)} %bitcast.19), channel_id=1, replica_groups=mesh['mem'=64,'grp'=2] {'mem','grp'}, dimensions={0} | all-to-all | bytes 131072 | tf_op jit(solution)/shard_map/all_to_all | solution.py:355
  132.0 3.2 %merge.1 = bf16[2048,1024]{1,0:T(8,128)(2,1)} custom-call(f32[128,128]{1,0:T(8,128)S(1)} %bitcast.16, f32[2048,1024]{1,0:T(8,128)S(1)} %get-tuple-element.15.all_ref, f32[2048,1024]{1,0:T(8,128)S(1)} %get-tuple-element.16.pos_ref), custom_call_target="tpu_custom_call" | custom-call | tf_op jit(solution)/shard_map/merge/pallas_call | solution.py:278
  135.2 5.3 %all-to-all-start.3 = ((bf16[128,16,1024]{2,1,0:T(8,128)(2,1)}), bf16[128,16,1024]{2,1,0:T(8,128)(2,1)}, u32[]{:S(2)}, u32[]{:S(2)}) async-start(bf16[128,16,1024]{2,1,0:T(8,128)(2,1)} %bitcast.24), calls=%async_computation.3 | async-start | bytes 8388608 | tf_op jit(solution)/shard_map/all_to_all | solution.py:355
  141.1 0.1 reduce
  141.2 1.3 picker.1
  142.6 0.0 copy-start.1
  142.6 2.2 %copy-done.1 = bf16[2048,1024]{1,0:T(8,128)(2,1)S(1)} copy-done((bf16[2048,1024]{1,0:T(8,128)(2,1)S(1)}, bf16[2048,1024]{1,0:T(8,128)(2,1)}, u32[]{:S(2)}) %copy-start.1) | copy-done | bytes 4194328
  144.7 2.9 %enqueue.1 = bf16[2048,1024]{1,0:T(8,128)(2,1)} custom-call(s32[1]{0:T(128)S(6)} %copy.12.refs_0_, bf16[144,1024]{1,0:T(8,128)(2,1)S(1)} %copy-done.2, bf16[2048,1024]{1,0:T(8,128)(2,1)S(1)} %copy-done.1), custom_call_target="tpu_custom_call" | custom-call | tf_op jit(solution)/shard_map/enqueue/pallas_call | solution.py:339
  147.6 45.6 %all-to-all-done.3 = bf16[128,16,1024]{2,1,0:T(8,128)(2,1)} async-done(((bf16[128,16,1024]{2,1,0:T(8,128)(2,1)}), bf16[128,16,1024]{2,1,0:T(8,128)(2,1)}, u32[]{:S(2)}, u32[]{:S(2)}) %all-to-all-start.3) | async-done | bytes 4194336 | tf_op jit(solution)/shard_map/all_to_all | solution.py:355
  193.3 3.8 %convolution_add_fusion = f32[144,1024]{1,0:T(8,128)} fusion(bf16[144,2048]{1,0:T(8,128)(2,1)S(1)} %picker.1, bf16[2048,1024]{1,0:T(8,128)(2,1)} %bitcast.11, bf16[144,1024]{1,0:T(8,128)(2,1)S(1)} %copy-done.2, f32[144]{0:T(256)S(1)} %reduce), kind=kOutput, calls=%fused_computation | convolution fusion | flops 604422144 | bytes 5669440 | tf_op jit(solution)/shard_map/dot_general | solution.py:377
Async XLA Ops:
  3.2 67.4 %copy-start = (bf16[2048,1024]{1,0:T(8,128)(2,1)S(1)}, bf16[2048,1024]{1,0:T(8,128)(2,1)}, u32[]{:S(2)}) copy-start(bf16[2048,1024]{1,0:T(8,128)(2,1)} %refs_2_) | copy-start | bytes 12582916
  3.2 67.4 %copy-start.5 = (s32[2048]{0:T(1024)S(1)}, s32[2048]{0:T(1024)}, u32[]{:S(2)}) copy-start(s32[2048]{0:T(1024)} %param.11) | copy-start | bytes 24580
  70.6 44.7 %copy-start.2 = (bf16[144,1024]{1,0:T(8,128)(2,1)S(1)}, bf16[144,1024]{1,0:T(8,128)(2,1)}, u32[]{:S(2)}) copy-start(bf16[144,1024]{1,0:T(8,128)(2,1)} %refs_1_.1) | copy-start | bytes 884740
  70.6 44.7 %copy-start.3 = (bf16[144,1024]{1,0:T(8,128)(2,1)S(1)}, bf16[144,1024]{1,0:T(8,128)(2,1)}, u32[]{:S(2)}) copy-start(bf16[144,1024]{1,0:T(8,128)(2,1)} %query_ref.3) | copy-start | bytes 884740
  70.6 44.7 %copy-start.4 = (s32[18,3]{0,1:T(4,128)S(1)}, s32[18,3]{0,1:T(4,128)}, u32[]{:S(2)}) copy-start(s32[18,3]{0,1:T(4,128)} %param.12) | copy-start | bytes 652
  135.2 58.1 %all-to-all-start.3 = ((bf16[128,16,1024]{2,1,0:T(8,128)(2,1)}), bf16[128,16,1024]{2,1,0:T(8,128)(2,1)}, u32[]{:S(2)}, u32[]{:S(2)}) async-start(bf16[128,16,1024]{2,1,0:T(8,128)(2,1)} %bitcast.24), calls=%async_computation.3 | async-start | bytes 8388608 | tf_op jit(solution)/shard_map/all_to_all | solution.py:355
  142.6 2.2 %copy-start.1 = (bf16[2048,1024]{1,0:T(8,128)(2,1)S(1)}, bf16[2048,1024]{1,0:T(8,128)(2,1)}, u32[]{:S(2)}) copy-start(bf16[2048,1024]{1,0:T(8,128)(2,1)} %refs_2_) | copy-start | bytes 12582916

commit v4 on v3

--- a/solution.py
+++ b/solution.py
@@ -15,8 +15,9 @@
 OWNER_STEP = 512
 OWNER_SUB = 256
 OWNER_MIB = 26
-MERGE_STEP = 512
-MERGE_MIB = 16
+MERGE_STEP = 1024
+GRADIENT_CUTS = 4
+MERGE_MIB = 28
 EXACT = lax.Precision.HIGHEST
 
 
@@ -204,17 +205,19 @@
     )
     lane = iota((rows, LANES), 1)
     mine = (lane & 7) == (iota((rows, LANES), 0) & 7)
+    masks = [[jnp.where(down_count == s, match, 0.0) for s in range(CAP)] for match in down_match]
+    wide = jnp.dot(
+        jnp.concatenate([jnp.concatenate(mask, axis=1) for mask in masks], axis=0),
+        jnp.concatenate([jnp.where(stat_slot == s, stat, 0.0) for s in range(CAP)], axis=0),
+        precision=EXACT,
+        preferred_element_type=F32,
+    )
     maxima, alls, poss = [], [], []
     for k in range(fanout):
-        wide = jnp.zeros((rows, LANES), F32)
-        for s in range(CAP):
-            mask = jnp.where(down_count == s, down_match[k], 0.0)
-            wide = wide + jnp.dot(
-                mask, jnp.where(stat_slot == s, stat, 0.0), precision=EXACT, preferred_element_type=F32
-            )
+        part = wide[k * rows : (k + 1) * rows]
         for group, into in enumerate((maxima, alls, poss)):
             pick = mine & ((lane >> 4) == group)
-            into.append(jnp.sum(jnp.where(pick, wide, 0.0), axis=1, keepdims=True))
+            into.append(jnp.sum(jnp.where(pick, part, 0.0), axis=1, keepdims=True))
     top = own
     for value in maxima:
         top = jnp.maximum(top, value)
@@ -228,26 +231,21 @@
     loss_ref[...] = jnp.sum(jnp.where(iota(side, 0) == iota(side, 1), loss, 0.0), axis=0, keepdims=True)
     factor_ref[...] = own_weight * (1.0 / total_all - 1.0 / total_pos)
 
-    across_block = iota((1, rows), 1) >> 3
-    across_match = [
-        (targets(pairs_ref, k, across_block) == iota((LANES, rows), 0)).astype(F32) for k in range(fanout)
-    ]
-    earlier_across = ((iota(side, 0) >> 3) < (iota(side, 1) >> 3)) & ((iota(side, 0) & 7) == 0)
-    across_count = jnp.dot(
-        sum(across_match[1:], across_match[0]).astype(BF16),
-        earlier_across.astype(F32).astype(BF16),
+    values = []
+    for k in range(fanout):
+        factor_all = scales[k] / total_all
+        factor_pos = jnp.where(total_pos > 0.0, scales[k] / total_pos, 0.0)
+        for s in range(CAP):
+            value = jnp.where((lane >> 3) == s, factor_all, 0.0)
+            value = jnp.where((lane >> 3) == 2 + s, factor_pos, value)
+            values.append(jnp.where(mine, value, 0.0))
+    back_ref[...] = lax.dot_general(
+        jnp.concatenate([mask for pair in masks for mask in pair], axis=0),
+        jnp.concatenate(values, axis=0),
+        (((0,), (0,)), ((), ())),
+        precision=EXACT,
         preferred_element_type=F32,
     )
-    back = jnp.zeros((LANES, LANES), F32)
-    for k in range(fanout):
-        factor_all, factor_pos = scales[k] / total_all, scales[k] / total_pos
-        for s in range(CAP):
-            mask = jnp.where(across_count == s, across_match[k], 0.0)
-            value = jnp.where((lane >> 3) == s, factor_all, 0.0)
-            value = jnp.where((lane >> 3) == 2 + s, factor_pos, value)
-            value = jnp.where(mine, value, 0.0)
-            back = back + jnp.dot(mask, value, precision=EXACT, preferred_element_type=F32)
-    back_ref[...] = back
 
 
 def totals(pairs, queries, keys, stat):
@@ -311,6 +309,42 @@
         compiler_params=pltpu.CompilerParams(vmem_limit_bytes=16 * MIB),
         name="picker",
     )(pairs)
+
+
+def gradient_kernel(picked_ref, back_hbm, factor_ref, key_ref, out_ref, back_ref, sems):
+    cuts = sems.shape[0]
+    rows = back_ref.shape[0] // cuts
+
+    def fetch(j):
+        at = pl.ds(j * rows, rows)
+        return pltpu.make_async_copy(back_hbm.at[at], back_ref.at[at], sems.at[j])
+
+    parts = [fetch(j) for j in range(cuts)]
+    for part in parts:
+        part.start()
+    total = factor_ref[...] * key_ref[...].astype(F32)
+    for j in range(cuts):
+        parts[j].wait()
+        at = slice(j * rows, (j + 1) * rows)
+        total = total + jnp.dot(picked_ref[:, at], back_ref[at, :], preferred_element_type=F32)
+    out_ref[...] = total
+
+
+def gradient(picked, back, factor, keys):
+    return pl.pallas_call(
+        gradient_kernel,
+        in_specs=[
+            pl.BlockSpec(memory_space=pltpu.VMEM),
+            pl.BlockSpec(memory_space=pl.ANY),
+            pl.BlockSpec(memory_space=pltpu.VMEM),
+            pl.BlockSpec(memory_space=pltpu.VMEM),
+        ],
+        out_specs=pl.BlockSpec(memory_space=pltpu.VMEM),
+        out_shape=jax.ShapeDtypeStruct(keys.shape, F32),
+        scratch_shapes=[pltpu.VMEM(back.shape, BF16), pltpu.SemaphoreType.DMA((GRADIENT_CUTS,))],
+        compiler_params=pltpu.CompilerParams(vmem_limit_bytes=16 * MIB),
+        name="gradient",
+    )(picked, back, factor, keys)
 
 
 def enqueue_kernel(slots, offset_ref, key_ref, memory_ref, out_ref):
@@ -374,7 +408,7 @@
     back = exchange(back, 16)
     updated = enqueue(offset, keys, held)
     picked = picker(pairs, rows_dev, shards * 16)
-    grad = jnp.dot(picked, back, preferred_element_type=F32) + factor * keys.astype(F32)
+    grad = gradient(picked, back, factor, keys)
     return loss.reshape(rows_dev), grad, updated
 
 

time: 197 us -> 197 us (level)
  matrix products: 3.8 us -> 0 us
  Pallas kernels: 43.6 us -> 46.8 us
    dot_general x1 -> x0, matrix products: 3.8 us -> none  [body(): jnp.dot(picked, back, preferred_element_type=F32)]
    pallas_call x0 -> x1, Pallas kernels: none -> 3.36 us  [gradient(): pl.pallas_call(gradient_kernel, in_specs=[pl.BlockSpec(memory_space=pltpu...]
where the time goes in v4:
time: 197 us; the launch traced here: 196 us
  blocking collectives  95.1 us (48%)
  Pallas kernels  46.8 us (24%)
  waiting for transfers between devices  45.5 us (23%)
  starting transfers between devices  5.31 us (3%)
  local copies, waits for them, and re-layouts  2.21 us (1%)
    all_to_all x3, blocking collectives, deal(): return lax.all_to_all(groups, AXES, split_axis=0, concat_axis=0, tiled=True)  95.1 us
    all_to_all x1, waiting for transfers between devices, deal(): return lax.all_to_all(groups, AXES, split_axis=0, concat_axis=0, tiled=True)  45.5 us
    pallas_call x1, Pallas kernels, owner(): pl.pallas_call(owner_kernel, grid=(total // step,), in_specs=[pl.BlockSpe...  30.8 us
    all_to_all x1, starting transfers between devices, deal(): return lax.all_to_all(groups, AXES, split_axis=0, concat_axis=0, tiled=True)  5.31 us
  transfers between devices with their start and end apart: 1, of which 1 were waited for; matrix products, arithmetic and copies ran while one was open for 0% of the time, Pallas kernels for 2%

profile of v4, /device:TPU:1, one launch (start us, length us, event | category | flops | bytes accessed | tf_op | source)
XLA Modules:
  0.0 196.3 jit_solution(4511951592687972197)
XLA Ops:
  0.6 2.6 %pack.1 = bf16[128,136,128]{2,1,0:T(8,128)(2,1)S(1)} custom-call(s32[3,18]{1,0:T(4,128)} %bitcast.18, s32[1,144]{1,0:T(1,128)} %bitcast.23, bf16[144,1024]{1,0:T(8,128)(2,1)} %query_ref.3), custom_call_target="tpu_custom_call" | custom-call | tf_op jit(solution)/shard_map/pack/pallas_call | solution.py:96
  3.2 0.0 copy-start
  3.2 0.0 copy-start.5
  3.2 67.3 %all_to_all.20.query_ref = bf16[128,136,128]{2,1,0:T(8,128)(2,1)S(1)} all-to-all(bf16[128,136,128]{2,1,0:T(8,128)(2,1)S(1)} %pack.1), channel_id=1, replica_groups=mesh['mem'=64,'grp'=2] {'mem','grp'}, dimensions={0} | all-to-all | bytes 8912896 | tf_op jit(solution)/shard_map/all_to_all | solution.py:389
  70.6 0.0 copy-done
  70.6 0.0 copy-done.5
  70.6 0.0 copy-start.2
  70.6 0.0 copy-start.3
  70.6 0.0 copy-start.4
  70.6 30.8 %owner.1 = (f32[2048,1024]{1,0:T(8,128)S(1)}, f32[2048,1024]{1,0:T(8,128)S(1)}, f32[128,128]{1,0:T(8,128)S(1)}) custom-call(bf16[128,136,128]{2,1,0:T(8,128)(2,1)S(1)} %all_to_all.20.query_ref, bf16[2048,1024]{1,0:T(8,128)(2,1)S(1)} %copy-done, s32[1,2048]{1,0:T(1,128)S(1)} %bitcast.21), custom_call_target="tpu_custom_call" | custom-call | flops 25769803776 | bytes 25165824 | tf_op jit(solution)/shard_map/owner/pallas_call | solution.py:162
  101.4 13.8 %all_to_all.21 = f32[128,1,128]{2,1,0:T(1,128)S(1)} all-to-all(f32[128,1,128]{2,1,0:T(1,128)S(1)} %bitcast.16), channel_id=1, replica_groups=mesh['mem'=64,'grp'=2] {'mem','grp'}, dimensions={0} | all-to-all | bytes 131072 | tf_op jit(solution)/shard_map/all_to_all | solution.py:389
  115.3 0.0 copy-done.2
  115.3 0.0 copy-done.3
  115.3 0.0 copy-done.4
  115.3 2.8 %totals.1 = (f32[1,144]{1,0:T(1,128)}, f32[144,1]{1,0:T(8,128)S(1)}, f32[128,128]{1,0:T(8,128)S(1)}) custom-call(s32[3,18]{1,0:T(4,128)S(1)} %bitcast.19, bf16[144,1024]{1,0:T(8,128)(2,1)S(1)} %copy-done.3, bf16[144,1024]{1,0:T(8,128)(2,1)S(1)} %copy-done.2, f32[128,128]{1,0:T(8,128)S(1)} %bitcast.15), custom_call_target="tpu_custom_call" | custom-call | tf_op jit(solution)/shard_map/totals/pallas_call | solution.py:253
  118.1 13.9 %all_to_all.22 = f32[128,1,128]{2,1,0:T(1,128)S(1)} all-to-all(f32[128,1,128]{2,1,0:T(1,128)S(1)} %bitcast.17), channel_id=1, replica_groups=mesh['mem'=64,'grp'=2] {'mem','grp'}, dimensions={0} | all-to-all | bytes 131072 | tf_op jit(solution)/shard_map/all_to_all | solution.py:389
  132.0 2.8 %merge.1 = bf16[2048,1024]{1,0:T(8,128)(2,1)} custom-call(f32[128,128]{1,0:T(8,128)S(1)} %bitcast.14, f32[2048,1024]{1,0:T(8,128)S(1)} %get-tuple-element.15.all_ref, f32[2048,1024]{1,0:T(8,128)S(1)} %get-tuple-element.16.pos_ref), custom_call_target="tpu_custom_call" | custom-call | tf_op jit(solution)/shard_map/merge/pallas_call | solution.py:276
  134.9 5.3 %all-to-all-start.3 = ((bf16[128,16,1024]{2,1,0:T(8,128)(2,1)}), bf16[128,16,1024]{2,1,0:T(8,128)(2,1)}, u32[]{:S(2)}, u32[]{:S(2)}) async-start(bf16[128,16,1024]{2,1,0:T(8,128)(2,1)} %bitcast.22), calls=%async_computation.3 | async-start | bytes 8388608 | tf_op jit(solution)/shard_map/all_to_all | solution.py:389
  140.8 1.3 picker.1.picked_ref
  142.2 0.0 copy-start.1
  142.2 2.2 %copy-done.1 = bf16[2048,1024]{1,0:T(8,128)(2,1)S(1)} copy-done((bf16[2048,1024]{1,0:T(8,128)(2,1)S(1)}, bf16[2048,1024]{1,0:T(8,128)(2,1)}, u32[]{:S(2)}) %copy-start.1) | copy-done | bytes 4194328
  144.4 3.1 %enqueue.1 = bf16[2048,1024]{1,0:T(8,128)(2,1)} custom-call(s32[1]{0:T(128)S(6)} %copy.12.refs_0_, bf16[144,1024]{1,0:T(8,128)(2,1)S(1)} %copy-done.2, bf16[2048,1024]{1,0:T(8,128)(2,1)S(1)} %copy-done.1), custom_call_target="tpu_custom_call" | custom-call | tf_op jit(solution)/shard_map/enqueue/pallas_call | solution.py:373
  147.4 45.5 %all-to-all-done.3 = bf16[128,16,1024]{2,1,0:T(8,128)(2,1)} async-done(((bf16[128,16,1024]{2,1,0:T(8,128)(2,1)}), bf16[128,16,1024]{2,1,0:T(8,128)(2,1)}, u32[]{:S(2)}, u32[]{:S(2)}) %all-to-all-start.3) | async-done | bytes 4194336 | tf_op jit(solution)/shard_map/all_to_all | solution.py:389
  193.0 3.4 %gradient.1 = f32[144,1024]{1,0:T(8,128)} custom-call(bf16[144,2048]{1,0:T(8,128)(2,1)S(1)} %picker.1.picked_ref, bf16[2048,1024]{1,0:T(8,128)(2,1)} %bitcast.11.back_hbm, f32[144,1]{1,0:T(8,128)S(1)} %get-tuple-element.19.factor_ref, bf16[144,1024]{1,0:T(8,128)(2,1)S(1)} %copy-done.2), custom_call_target="tpu_custom_call" | custom-call | tf_op jit(solution)/shard_map/gradient/pallas_call | solution.py:334
Async XLA Ops:
  3.2 67.4 %copy-start = (bf16[2048,1024]{1,0:T(8,128)(2,1)S(1)}, bf16[2048,1024]{1,0:T(8,128)(2,1)}, u32[]{:S(2)}) copy-start(bf16[2048,1024]{1,0:T(8,128)(2,1)} %refs_2_) | copy-start | bytes 12582916
  3.2 67.4 %copy-start.5 = (s32[2048]{0:T(1024)S(1)}, s32[2048]{0:T(1024)}, u32[]{:S(2)}) copy-start(s32[2048]{0:T(1024)} %param.11) | copy-start | bytes 24580
  70.6 44.7 %copy-start.2 = (bf16[144,1024]{1,0:T(8,128)(2,1)S(1)}, bf16[144,1024]{1,0:T(8,128)(2,1)}, u32[]{:S(2)}) copy-start(bf16[144,1024]{1,0:T(8,128)(2,1)} %refs_1_.1) | copy-start | bytes 884740
  70.6 44.7 %copy-start.3 = (bf16[144,1024]{1,0:T(8,128)(2,1)S(1)}, bf16[144,1024]{1,0:T(8,128)(2,1)}, u32[]{:S(2)}) copy-start(bf16[144,1024]{1,0:T(8,128)(2,1)} %query_ref.3) | copy-start | bytes 884740
  70.6 44.7 %copy-start.4 = (s32[18,3]{0,1:T(4,128)S(1)}, s32[18,3]{0,1:T(4,128)}, u32[]{:S(2)}) copy-start(s32[18,3]{0,1:T(4,128)} %param.12) | copy-start | bytes 652
  134.9 58.1 %all-to-all-start.3 = ((bf16[128,16,1024]{2,1,0:T(8,128)(2,1)}), bf16[128,16,1024]{2,1,0:T(8,128)(2,1)}, u32[]{:S(2)}, u32[]{:S(2)}) async-start(bf16[128,16,1024]{2,1,0:T(8,128)(2,1)} %bitcast.22), calls=%async_computation.3 | async-start | bytes 8388608 | tf_op jit(solution)/shard_map/all_to_all | solution.py:389
  142.2 2.2 %copy-start.1 = (bf16[2048,1024]{1,0:T(8,128)(2,1)S(1)}, bf16[2048,1024]{1,0:T(8,128)(2,1)}, u32[]{:S(2)}) copy-start(bf16[2048,1024]{1,0:T(8,128)(2,1)} %refs_2_) | copy-start | bytes 12582916

commit v5 on v4

--- a/solution.py
+++ b/solution.py
@@ -12,7 +12,7 @@
 AXES = ("mem", "grp")
 LANES = 128
 MIB = 1024 * 1024
-OWNER_STEP = 512
+OWNER_STEP = 2048
 OWNER_SUB = 256
 OWNER_MIB = 26
 MERGE_STEP = 1024
@@ -114,8 +114,9 @@
 def owner_kernel(query_ref, memory_ref, slot_label_ref, all_ref, pos_ref, stat_ref):
     width = memory_ref.shape[1]
     sub = OWNER_SUB
+    lead = pl.program_id(0) * OWNER_STEP
     for c in range(OWNER_STEP // sub):
-        at = slice(c * sub, (c + 1) * sub)
+        at = pl.ds(pl.multiple_of(lead + c * sub, sub), sub)
         places = slice(c * sub // 16, (c + 1) * sub // 16)
         query = jnp.concatenate(
             [
@@ -168,13 +169,13 @@
             pl.BlockSpec((1, slots), lambda i: (0, 0)),
         ],
         out_specs=[
-            pl.BlockSpec((step, width), lambda i: (i, 0)),
-            pl.BlockSpec((step, width), lambda i: (i, 0)),
+            pl.BlockSpec(memory_space=pltpu.VMEM),
+            pl.BlockSpec(memory_space=pltpu.VMEM),
             pl.BlockSpec((step // 16, LANES), lambda i: (i, 0)),
         ],
         out_shape=[
-            jax.ShapeDtypeStruct((total, width), F32),
-            jax.ShapeDtypeStruct((total, width), F32),
+            pltpu.VMEM((total, width), F32),
+            pltpu.VMEM((total, width), F32),
             jax.ShapeDtypeStruct((total // 16, LANES), F32),
         ],
         compiler_params=pltpu.CompilerParams(vmem_limit_bytes=OWNER_MIB * MIB),

time: 197 us -> 195 us (0.990)
  no operation moved by 1% of the time
where the time goes in v5:
time: 195 us
  blocking collectives  95.1 us (49%)
  waiting for transfers between devices  45.5 us (23%)
  Pallas kernels  45.2 us (23%)
  starting transfers between devices  5.31 us (3%)
  local copies, waits for them, and re-layouts  2.21 us (1%)
    all_to_all x3, blocking collectives, deal(): return lax.all_to_all(groups, AXES, split_axis=0, concat_axis=0, tiled=True)  95.1 us
    all_to_all x1, waiting for transfers between devices, deal(): return lax.all_to_all(groups, AXES, split_axis=0, concat_axis=0, tiled=True)  45.5 us
    pallas_call x1, Pallas kernels, owner(): pl.pallas_call(owner_kernel, grid=(total // step,), in_specs=[pl.BlockSpe...  29.2 us
    all_to_all x1, starting transfers between devices, deal(): return lax.all_to_all(groups, AXES, split_axis=0, concat_axis=0, tiled=True)  5.31 us
  transfers between devices with their start and end apart: 1, of which 1 were waited for; matrix products, arithmetic and copies ran while one was open for 0% of the time, Pallas kernels for 2%

profile of v5, /device:TPU:1, one launch (start us, length us, event | category | flops | bytes accessed | tf_op | source)
XLA Modules:
  0.0 194.9 jit_solution(2583549378281864585)
XLA Ops:
  0.6 2.6 %pack.1 = bf16[128,136,128]{2,1,0:T(8,128)(2,1)S(1)} custom-call(s32[3,18]{1,0:T(4,128)} %bitcast.18, s32[1,144]{1,0:T(1,128)} %bitcast.23, bf16[144,1024]{1,0:T(8,128)(2,1)} %query_ref.3), custom_call_target="tpu_custom_call" | custom-call | tf_op jit(solution)/shard_map/pack/pallas_call | solution.py:96
  3.2 0.0 copy-start
  3.2 0.0 copy-start.5
  3.2 67.3 %all_to_all.20.query_ref = bf16[128,136,128]{2,1,0:T(8,128)(2,1)S(1)} all-to-all(bf16[128,136,128]{2,1,0:T(8,128)(2,1)S(1)} %pack.1), channel_id=1, replica_groups=mesh['mem'=64,'grp'=2] {'mem','grp'}, dimensions={0} | all-to-all | bytes 8912896 | tf_op jit(solution)/shard_map/all_to_all | solution.py:390
  70.6 0.0 copy-done
  70.6 0.0 copy-done.5
  70.6 0.0 copy-start.2
  70.6 0.0 copy-start.3
  70.6 0.0 copy-start.4
  70.6 29.2 %owner.1 = (f32[2048,1024]{1,0:T(8,128)S(1)}, f32[2048,1024]{1,0:T(8,128)S(1)}, f32[128,128]{1,0:T(8,128)S(1)}) custom-call(bf16[128,136,128]{2,1,0:T(8,128)(2,1)S(1)} %all_to_all.20.query_ref, bf16[2048,1024]{1,0:T(8,128)(2,1)S(1)} %copy-done, s32[1,2048]{1,0:T(1,128)S(1)} %bitcast.21), custom_call_target="tpu_custom_call" | custom-call | flops 25769803776 | bytes 25165824 | tf_op jit(solution)/shard_map/owner/pallas_call | solution.py:163
  99.8 13.9 %all_to_all.21 = f32[128,1,128]{2,1,0:T(1,128)S(1)} all-to-all(f32[128,1,128]{2,1,0:T(1,128)S(1)} %bitcast.16), channel_id=1, replica_groups=mesh['mem'=64,'grp'=2] {'mem','grp'}, dimensions={0} | all-to-all | bytes 131072 | tf_op jit(solution)/shard_map/all_to_all | solution.py:390
  113.6 0.0 copy-done.2
  113.7 0.0 copy-done.3
  113.7 0.0 copy-done.4
  113.7 2.8 %totals.1 = (f32[1,144]{1,0:T(1,128)}, f32[144,1]{1,0:T(8,128)S(1)}, f32[128,128]{1,0:T(8,128)S(1)}) custom-call(s32[3,18]{1,0:T(4,128)S(1)} %bitcast.19, bf16[144,1024]{1,0:T(8,128)(2,1)S(1)} %copy-done.3, bf16[144,1024]{1,0:T(8,128)(2,1)S(1)} %copy-done.2, f32[128,128]{1,0:T(8,128)S(1)} %bitcast.15), custom_call_target="tpu_custom_call" | custom-call | tf_op jit(solution)/shard_map/totals/pallas_call | solution.py:254
  116.5 13.9 %all_to_all.22 = f32[128,1,128]{2,1,0:T(1,128)S(1)} all-to-all(f32[128,1,128]{2,1,0:T(1,128)S(1)} %bitcast.17), channel_id=1, replica_groups=mesh['mem'=64,'grp'=2] {'mem','grp'}, dimensions={0} | all-to-all | bytes 131072 | tf_op jit(solution)/shard_map/all_to_all | solution.py:390
  130.4 2.8 %merge.1 = bf16[2048,1024]{1,0:T(8,128)(2,1)} custom-call(f32[128,128]{1,0:T(8,128)S(1)} %bitcast.14, f32[2048,1024]{1,0:T(8,128)S(1)} %get-tuple-element.15.all_ref, f32[2048,1024]{1,0:T(8,128)S(1)} %get-tuple-element.16.pos_ref), custom_call_target="tpu_custom_call" | custom-call | tf_op jit(solution)/shard_map/merge/pallas_call | solution.py:277
  133.3 5.3 %all-to-all-start.3 = ((bf16[128,16,1024]{2,1,0:T(8,128)(2,1)}), bf16[128,16,1024]{2,1,0:T(8,128)(2,1)}, u32[]{:S(2)}, u32[]{:S(2)}) async-start(bf16[128,16,1024]{2,1,0:T(8,128)(2,1)} %bitcast.22), calls=%async_computation.3 | async-start | bytes 8388608 | tf_op jit(solution)/shard_map/all_to_all | solution.py:390
  139.2 1.3 picker.1.picked_ref
  140.5 0.0 copy-start.1
  140.5 2.2 %copy-done.1 = bf16[2048,1024]{1,0:T(8,128)(2,1)S(1)} copy-done((bf16[2048,1024]{1,0:T(8,128)(2,1)S(1)}, bf16[2048,1024]{1,0:T(8,128)(2,1)}, u32[]{:S(2)}) %copy-start.1) | copy-done | bytes 4194328
  142.7 3.1 %enqueue.1 = bf16[2048,1024]{1,0:T(8,128)(2,1)} custom-call(s32[1]{0:T(128)S(6)} %copy.12.refs_0_, bf16[144,1024]{1,0:T(8,128)(2,1)S(1)} %copy-done.2, bf16[2048,1024]{1,0:T(8,128)(2,1)S(1)} %copy-done.1), custom_call_target="tpu_custom_call" | custom-call | tf_op jit(solution)/shard_map/enqueue/pallas_call | solution.py:374
  145.8 45.5 %all-to-all-done.3 = bf16[128,16,1024]{2,1,0:T(8,128)(2,1)} async-done(((bf16[128,16,1024]{2,1,0:T(8,128)(2,1)}), bf16[128,16,1024]{2,1,0:T(8,128)(2,1)}, u32[]{:S(2)}, u32[]{:S(2)}) %all-to-all-start.3) | async-done | bytes 4194336 | tf_op jit(solution)/shard_map/all_to_all | solution.py:390
  191.3 3.4 %gradient.1 = f32[144,1024]{1,0:T(8,128)} custom-call(bf16[144,2048]{1,0:T(8,128)(2,1)S(1)} %picker.1.picked_ref, bf16[2048,1024]{1,0:T(8,128)(2,1)} %bitcast.11.back_hbm, f32[144,1]{1,0:T(8,128)S(1)} %get-tuple-element.19.factor_ref, bf16[144,1024]{1,0:T(8,128)(2,1)S(1)} %copy-done.2), custom_call_target="tpu_custom_call" | custom-call | tf_op jit(solution)/shard_map/gradient/pallas_call | solution.py:335
Async XLA Ops:
  3.2 67.4 %copy-start = (bf16[2048,1024]{1,0:T(8,128)(2,1)S(1)}, bf16[2048,1024]{1,0:T(8,128)(2,1)}, u32[]{:S(2)}) copy-start(bf16[2048,1024]{1,0:T(8,128)(2,1)} %refs_2_) | copy-start | bytes 12582916
  3.2 67.4 %copy-start.5 = (s32[2048]{0:T(1024)S(1)}, s32[2048]{0:T(1024)}, u32[]{:S(2)}) copy-start(s32[2048]{0:T(1024)} %param.11) | copy-start | bytes 24580
  70.6 43.1 %copy-start.2 = (bf16[144,1024]{1,0:T(8,128)(2,1)S(1)}, bf16[144,1024]{1,0:T(8,128)(2,1)}, u32[]{:S(2)}) copy-start(bf16[144,1024]{1,0:T(8,128)(2,1)} %refs_1_.1) | copy-start | bytes 884740
  70.6 43.1 %copy-start.3 = (bf16[144,1024]{1,0:T(8,128)(2,1)S(1)}, bf16[144,1024]{1,0:T(8,128)(2,1)}, u32[]{:S(2)}) copy-start(bf16[144,1024]{1,0:T(8,128)(2,1)} %query_ref.3) | copy-start | bytes 884740
  70.6 43.1 %copy-start.4 = (s32[18,3]{0,1:T(4,128)S(1)}, s32[18,3]{0,1:T(4,128)}, u32[]{:S(2)}) copy-start(s32[18,3]{0,1:T(4,128)} %param.12) | copy-start | bytes 652
  133.3 58.1 %all-to-all-start.3 = ((bf16[128,16,1024]{2,1,0:T(8,128)(2,1)}), bf16[128,16,1024]{2,1,0:T(8,128)(2,1)}, u32[]{:S(2)}, u32[]{:S(2)}) async-start(bf16[128,16,1024]{2,1,0:T(8,128)(2,1)} %bitcast.22), calls=%async_computation.3 | async-start | bytes 8388608 | tf_op jit(solution)/shard_map/all_to_all | solution.py:390
  140.5 2.2 %copy-start.1 = (bf16[2048,1024]{1,0:T(8,128)(2,1)S(1)}, bf16[2048,1024]{1,0:T(8,128)(2,1)}, u32[]{:S(2)}) copy-start(bf16[2048,1024]{1,0:T(8,128)(2,1)} %refs_2_) | copy-start | bytes 12582916
